TPU v7x, 128 devices: a whole 4x4x4 slice. The times are simulated.
128 devices in a mesh: ep: 4 (over x), edp: 32 (over z, y, core).
Axes of the slice: x: 4, y: 4, z: 4, core: 2. Of those that a mesh axis runs over, the one named last changes fastest.
Arguments:
- out_grad: bfloat16 [131072, 4096], P(('ep', 'edp')), may hold values from -6 to 6
- block_target: int32 [1024, 1], P(('ep', 'edp')), may hold values from 0 to 3; in each aligned block of 8 rows (0 to 7, 8 to 15, ...) at most 4 rows name the same one
- saved_hidden: bfloat16 [262144, 768], P(('ep', 'edp')), may hold values from -24 to 24
- master_weight: float32 [4, 768, 4096], P('ep', 'edp'), may hold values from -4 to 4
- first_moment: float32 [4, 768, 4096], P('ep', 'edp'), may hold values from -3 to 3
- second_moment: float32 [4, 768, 4096], P('ep', 'edp'), may hold values from 0.01 to 1
Outputs:
- hidden_grad: bfloat16 [131072, 768], P(('ep', 'edp'))
- new_weight: float32 [4, 768, 4096], P('ep', 'edp')
- new_first: float32 [4, 768, 4096], P('ep', 'edp')
- new_second: float32 [4, 768, 4096], P('ep', 'edp')
Inputs may be any that keep to these rules, and one draw needn't show every extreme that they name: `block_target`: of one device's 8 blocks at most 4 go to one expert; in every draw some device sends exactly 4 blocks to some expert.
All inputs are finite; a program needn't handle non-finite values.
Results may differ from a plain program's by a relative error of at most 0.014.
Values may be sent and summed in bfloat16 or wider, within the bound.
A program may use at most 128 MiB of HBM per device.

v0:
```python
import jax
import jax.numpy as jnp
from jax import lax
from jax.sharding import PartitionSpec as P

BLOCK = 128
STEP = 1000


BETA_ONE = 0.9
BETA_TWO = 0.999
LEARN_RATE = 0.01
EPSILON = 1e-08


def body(out_grad, block_target, saved_hidden, master_weight, first_moment, second_moment):
    experts = lax.axis_size("ep")
    rows_local, model_width = out_grad.shape
    blocks = rows_local // BLOCK
    capacity = saved_hidden.shape[0] // (experts * BLOCK)
    factor = model_width ** (-0.5)
    target = block_target[:, 0]
    onehot = (target[:, None] == jnp.arange(experts, dtype=jnp.int32)[None, :]).astype(jnp.int32)
    earlier = jnp.cumsum(onehot, axis=0) - onehot
    slot_rank = jnp.sum(earlier * onehot, axis=1)
    slot_code = target * capacity + slot_rank
    selector = (
        jnp.arange(experts * capacity, dtype=jnp.int32)[:, None] == slot_code[None, :]
    ).astype(jnp.bfloat16)
    grad_blocks = out_grad.reshape(blocks, BLOCK * model_width)
    outbound = jnp.dot(selector, grad_blocks, preferred_element_type=jnp.float32).astype(
        jnp.bfloat16
    )
    outbound = outbound.reshape(experts, capacity, BLOCK, model_width)
    weight_low = master_weight.astype(jnp.bfloat16)
    received = lax.all_to_all(outbound, "ep", split_axis=0, concat_axis=0, tiled=True)
    flat_rows = received.reshape(-1, model_width)
    product = lax.dot_general(
        flat_rows,
        lax.all_gather(weight_low, "edp", axis=1, tiled=True)[0],
        (((1,), (1,)), ((), ())),
        preferred_element_type=jnp.float32,
    )
    hidden_slots = (product * factor).astype(jnp.bfloat16)
    returned = lax.all_to_all(
        hidden_slots.reshape(experts, capacity, BLOCK, -1),
        "ep",
        split_axis=0,
        concat_axis=0,
        tiled=True,
    )
    returned_flat = returned.reshape(experts * capacity, -1)
    hidden_grad = lax.dot_general(
        selector, returned_flat, (((0,), (0,)), ((), ())), preferred_element_type=jnp.float32
    )
    hidden_grad = hidden_grad.astype(jnp.bfloat16).reshape(rows_local, -1)
    grad_term = (
        lax.dot_general(
            saved_hidden, flat_rows, (((0,), (0,)), ((), ())), preferred_element_type=jnp.float32
        )
        * factor
    )
    weight_grad = lax.psum_scatter(
        grad_term.astype(jnp.bfloat16), "edp", scatter_dimension=0, tiled=True
    ).astype(jnp.float32)
    weight_grad = weight_grad[None]
    new_first = BETA_ONE * first_moment + (1.0 - BETA_ONE) * weight_grad
    new_second = BETA_TWO * second_moment + (1.0 - BETA_TWO) * weight_grad * weight_grad
    first_fix = 1.0 - BETA_ONE**STEP
    second_fix = 1.0 - BETA_TWO**STEP
    new_weight = master_weight - LEARN_RATE * (new_first / first_fix) / (
        jnp.sqrt(new_second / second_fix) + EPSILON
    )
    return (hidden_grad, new_weight, new_first, new_second)


def solution(mesh):
    placed = (
        P(("ep", "edp"), None),
        P(("ep", "edp"), None),
        P(("ep", "edp"), None),
        P("ep", "edp", None),
        P("ep", "edp", None),
        P("ep", "edp", None),
    )
    return jax.shard_map(
        body,
        mesh=mesh,
        in_specs=placed,
        out_specs=(
            P(("ep", "edp"), None),
            P("ep", "edp", None),
            P("ep", "edp", None),
            P("ep", "edp", None),
        ),
        check_vma=False,
    )
```

profile of v0, /device:TPU:1, one launch (start us, length us, event | category | flops | bytes accessed | tf_op | source)
XLA Modules:
  0.0 478.7 jit_solution(11653908944020445545)
XLA Ops:
  7.2 0.0 copy-start
  7.2 0.0 reduce-scatter.4.cloned.1.call-start
  7.2 0.8 fusion.11
  8.0 0.2 reduce_window_sum.11
  8.2 0.7 select_reduce_fusion
  8.9 0.7 multiply_add_fusion
  9.6 10.4 %reshape.37 = bf16[8,524288]{1,0:T(8,128)(2,1)} reshape(bf16[1024,4096]{1,0:T(8,128)(2,1)} %param.6) | data formatting | bytes 16777216 | tf_op jit(solution)/shard_map/reshape | solution.py:30
  19.9 11.4 %convolution_convert_fusion = bf16[16,524288]{1,0:T(8,128)(2,1)} fusion(bf16[8,524288]{1,0:T(8,128)(2,1)} %reshape.37, s32[8]{0:T(128)S(1)} %multiply_add_fusion), kind=kOutput, calls=%fused_computation | convolution fusion | flops 142606464 | bytes 25165856 | tf_op jit(solution)/shard_map/dot_general | solution.py:31
  31.4 14.7 %copy.31 = bf16[2,8,128,4096]{3,2,1,0:T(8,128)(2,1)S(1)} copy(bf16[2,8,128,4096]{3,1,2,0:T(8,128)(2,1)} %bitcast.33) | data formatting | bytes 33554432
  46.1 187.4 %all_to_all.10 = bf16[4,4,128,4096]{3,2,1,0:T(8,128)(2,1)S(1)} all-to-all(bf16[4,4,128,4096]{3,2,1,0:T(8,128)(2,1)S(1)} %bitcast.34), channel_id=1, replica_groups=mesh['ep'=4,'edp'=32] {'ep'}, dimensions={0} | all-to-all | bytes 33554432 | tf_op jit(solution)/shard_map/all_to_all | solution.py:36
  233.4 0.0 copy-start.2
  233.4 5.7 %copy-done.2 = bf16[4,4,128,4096]{3,2,1,0:T(8,128)(2,1)} copy-done((bf16[4,4,128,4096]{3,2,1,0:T(8,128)(2,1)}, bf16[4,4,128,4096]{3,2,1,0:T(8,128)(2,1)S(1)}, u32[]{:S(2)}) %copy-start.2) | copy-done | bytes 16777240
  239.2 0.0 copy-done
  239.2 17.8 %fusion.2 = bf16[768,4096]{0,1:T(8,128)(2,1)} fusion(bf16[2048,4096]{1,0:T(8,128)(2,1)S(1)} %bitcast.36, bf16[2048,768]{1,0:T(8,128)(2,1)S(1)} %copy-done), kind=kOutput, calls=%fused_computation.6 | convolution fusion | flops 12891193344 | bytes 26214400 | tf_op jit(solution)/shard_map/dot_general | solution.py:58
  256.9 8.8 %copy.29 = bf16[768,4096]{1,0:T(8,128)(2,1)} copy(bf16[768,4096]{0,1:T(8,128)(2,1)} %fusion.2) | data formatting | bytes 12582912
  265.7 0.0 copy-start.4
  265.7 0.0 copy-start.5
  265.7 0.0 reduce-scatter.4.cloned.1.call-update
  265.7 0.0 all-gather.2.cloned.1.call-start
  265.7 86.6 %reduce-scatter.4.cloned.1.call-done = bf16[24,4096]{1,0:T(8,128)(2,1)} async-done(((bf16[768,4096]{1,0:T(8,128)(2,1)}), bf16[24,4096]{1,0:T(8,128)(2,1)}) %reduce-scatter.4.cloned.1.call-update) | async-done | bytes 196624 | tf_op jit(solution)/shard_map/reduce_scatter | solution.py:63
  352.3 0.0 copy-done.3
  352.3 0.0 copy-done.4
  352.3 0.0 copy-done.5
  352.3 2.2 divide_subtract_fusion
  354.5 0.0 all-gather.2.cloned.1.call-update
  354.5 51.5 %all-gather.2.cloned.1.call-done = bf16[1,768,4096]{2,1,0:T(8,128)(2,1)} async-done(((bf16[1,24,4096]{2,1,0:T(8,128)(2,1)}), bf16[1,768,4096]{2,1,0:T(8,128)(2,1)}) %all-gather.2.cloned.1.call-update) | async-done | bytes 6291472 | tf_op jit(solution)/shard_map/all_gather | solution.py:40
  406.0 18.2 %multiply_convert_fusion.1 = bf16[2048,768]{1,0:T(8,128)(2,1)S(1)} fusion(bf16[2048,4096]{1,0:T(8,128)(2,1)} %bitcast.37, bf16[1,768,4096]{2,1,0:T(8,128)(2,1)} %all-gather.2.cloned.1.call-done), kind=kOutput, calls=%fused_computation.5 | convolution fusion | flops 12888047616 | bytes 26214400 | tf_op jit(solution)/shard_map/dot_general | solution.py:38
  424.2 40.9 %all_to_all.11 = bf16[4,4,128,768]{3,2,1,0:T(8,128)(2,1)S(1)} all-to-all(bf16[4,4,128,768]{3,2,1,0:T(8,128)(2,1)S(1)} %bitcast.39), channel_id=1, replica_groups=mesh['ep'=4,'edp'=32] {'ep'}, dimensions={0} | all-to-all | bytes 6291456 | tf_op jit(solution)/shard_map/all_to_all | solution.py:45
  465.0 1.7 copy.32
  466.8 1.8 convolution_convert_fusion.1
  468.6 3.3 reshape.42
  471.8 0.0 copy-done.1
  (2 shorter events, 0.0 us)
Async XLA Ops:
  7.2 232.0 %copy-start = (bf16[2048,768]{1,0:T(8,128)(2,1)S(1)}, bf16[2048,768]{1,0:T(8,128)(2,1)}, u32[]{:S(2)}) copy-start(bf16[2048,768]{1,0:T(8,128)(2,1)} %param.8) | copy-start | bytes 9437188
  7.2 345.1 %reduce-scatter.4.cloned.1.call-start = ((), (), s32[]{:S(2)}) async-start(), calls=%async_computation.4 | async-start | bytes 6488064 | tf_op jit(solution)/shard_map/reduce_scatter | solution.py:63
  233.4 5.7 %copy-start.2 = (bf16[4,4,128,4096]{3,2,1,0:T(8,128)(2,1)}, bf16[4,4,128,4096]{3,2,1,0:T(8,128)(2,1)S(1)}, u32[]{:S(2)}) copy-start(bf16[4,4,128,4096]{3,2,1,0:T(8,128)(2,1)S(1)} %all_to_all.10) | copy-start | bytes 50331652
  265.7 86.7 %copy-start.3 = (f32[1,24,4096]{2,1,0:T(8,128)S(1)}, f32[1,24,4096]{2,1,0:T(8,128)}, u32[]{:S(2)}) copy-start(f32[1,24,4096]{2,1,0:T(8,128)} %param.9) | copy-start | bytes 1179652
  265.7 86.7 %copy-start.4 = (f32[1,24,4096]{2,1,0:T(8,128)S(1)}, f32[1,24,4096]{2,1,0:T(8,128)}, u32[]{:S(2)}) copy-start(f32[1,24,4096]{2,1,0:T(8,128)} %param.10) | copy-start | bytes 1179652
  265.7 86.7 %copy-start.5 = (f32[1,24,4096]{2,1,0:T(8,128)S(1)}, f32[1,24,4096]{2,1,0:T(8,128)}, u32[]{:S(2)}) copy-start(f32[1,24,4096]{2,1,0:T(8,128)} %param.11) | copy-start | bytes 1179652
  265.7 140.3 %all-gather.2.cloned.1.call-start = ((), (), s32[]{:S(2)}) async-start(), calls=%async_computation.3 | async-start | bytes 6488064 | tf_op jit(solution)/shard_map/all_gather | solution.py:40
  465.0 6.8 %copy-start.1 = (bf16[2048,768]{1,0:T(8,128)(2,1)S(1)}, bf16[2048,768]{1,0:T(8,128)(2,1)}, u32[]{:S(2)}) copy-start(bf16[2048,768]{1,0:T(8,128)(2,1)} %param.8) | copy-start | bytes 9437188
Sparse Core Ops, SparseCore 0:
  265.8 86.4 reduce-scatter.3
  355.4 50.5 all-gather.1
where the time goes:
time: 479 us
  blocking collectives  228 us (48%)
  waiting for transfers between devices  138 us (29%)
  matrix products  49.1 us (10%)
  local copies, waits for them, and re-layouts  44.6 us (9%)
  between operations  14.1 us (3%)
    all_to_all x1, blocking collectives, body(): lax.all_to_all(outbound, 'ep', split_axis=0, concat_axis=0, tiled=True)  187 us
    reduce_scatter x1, waiting for transfers between devices, body(): lax.psum_scatter(grad_term.astype(jnp.bfloat16), 'edp', scatter_dimension...  86.6 us
    all_gather x1, waiting for transfers between devices, body(): lax.all_gather(weight_low, 'edp', axis=1, tiled=True)[0]  51.5 us
    all_to_all x1, blocking collectives, body(): lax.all_to_all(hidden_slots.reshape(experts, capacity, BLOCK, -1), 'ep',...  40.9 us
    unnamed x15, local copies, waits for them, and re-layouts  31 us
    dot_general x1, matrix products, body(): lax.dot_general(flat_rows, lax.all_gather(weight_low, 'edp', axis=1, tile...  18.2 us
    dot_general x1, matrix products, body(): lax.dot_general(saved_hidden, flat_rows, (((0,), (0,)), ((), ())), prefer...  17.8 us
    dot_general x1, matrix products, body(): jnp.dot(selector, grad_blocks, preferred_element_type=jnp.float32)  11.4 us
  transfers between devices with their start and end apart: 2, of which 2 were waited for; matrix products, arithmetic and copies ran while one was open for 0% of the time, Pallas kernels for 0%

commit v1 on v0

v1 whole, which is shorter than its diff:
```python
import jax
import jax.numpy as jnp
from jax import lax
from jax.experimental import pallas as pl
from jax.experimental.pallas import tpu as pltpu
from jax.sharding import PartitionSpec as P

MESH = pl.DeviceIdType.MESH
F32 = jnp.float32
BF16 = jnp.bfloat16

BLOCK = 128
STEP = 1000
BETA_ONE = 0.9
BETA_TWO = 0.999
LEARN_RATE = 0.01
EPSILON = 1e-08

RING = 4
EXPERTS = 4
CAP = 4
BLOCKS = 8
D = 4096
HALF = D // 2
FF = 768
ROWS = 48
X, Z, Y = 0, 1, 2
GROUPS = ((512, (Y, Z, X)), (768, (X, Y, Z)), (768, (X, Z, Y)))
OFFSETS = (0, 512, 1280)
NG = len(GROUPS)
TILE = 256


def kernel(og_hbm, bt_ref, sh_hbm, mw_hbm, hg_hbm, wg_ref, *scratch):
    it = iter(scratch)
    og = next(it)
    w = [next(it) for _ in range(NG)]
    part = [next(it) for _ in range(NG)]
    land = [[next(it) for _ in range(3)] for _ in range(NG)]
    hid = next(it)
    fwd = next(it)
    hid_t = next(it)
    wbuf = next(it)
    tgt = next(it)
    tsm = next(it)
    hsend = next(it)
    hrecv = next(it)
    fin = next(it)
    wgs = next(it)
    ag_s, ag_r, rs_s, rs_r = next(it), next(it), next(it), next(it)
    hs, hr, hcs, hcr = next(it), next(it), next(it), next(it)
    ms, mr = next(it), next(it)
    loc = next(it)
    hps, hpr, hos = next(it), next(it), next(it)

    x = lax.axis_index("ep")
    e = lax.axis_index("edp")
    c = lax.rem(e, 2)
    y = lax.rem(e // 2, RING)
    z = e // (2 * RING)
    oc = 1 - c
    mine = (x, z, y)

    def wrap(v):
        return lax.rem(v + RING, RING)

    def near(axis, delta):
        at = list(mine)
        at[axis] = wrap(at[axis] + delta)
        return (at[0], (at[1] * RING + at[2]) * 2 + c)

    other = (x, e + 1 - 2 * c)

    barrier = pltpu.get_barrier_semaphore()
    for axis in (X, Z, Y):
        for delta in (1, -1):
            pl.semaphore_signal(barrier, inc=1, device_id=near(axis, delta), device_id_type=MESH)
    pl.semaphore_signal(barrier, inc=1, device_id=other, device_id_type=MESH)
    tgt[c] = jnp.broadcast_to(bt_ref[...], (BLOCKS, 128))
    pl.semaphore_wait(barrier, 7)

    sent = []

    def remote(src, dst, s, r, dev):
        return pltpu.make_async_remote_copy(
            src_ref=src, dst_ref=dst, send_sem=s, recv_sem=r, device_id=dev, device_id_type=MESH
        )

    def push(*a):
        copy = remote(*a)
        copy.start()
        sent.append(copy)
        return copy

    def cols(who):
        return pl.ds(pl.multiple_of(who * HALF, HALF), HALF)

    def seg(who, n, start=0):
        return pl.ds(pl.multiple_of(who * CAP * BLOCK, CAP * BLOCK) + start, n)

    w_local = pltpu.make_async_copy(mw_hbm.at[0, :, cols(c)], wbuf.at[c], loc.at[0])
    w_local.start()
    w_peer = push(mw_hbm.at[0, :, cols(oc)], wbuf.at[c], ms.at[0], mr.at[0], other)
    t_peer = push(tgt.at[c], tgt.at[c], ms.at[1], mr.at[1], other)
    SEGR = CAP * BLOCK
    HS = SEGR // 2
    for d, delta in enumerate((1, -1)):
        push(sh_hbm.at[seg(wrap(x + 2), HS, d * HS)], fwd.at[d], hs.at[d, 0], hr.at[d, 0], near(X, delta))
    for d, delta in enumerate((1, -1)):
        push(sh_hbm.at[seg(wrap(x + delta), SEGR)], hid.at[c, x], hs.at[d, 1], hr.at[d, 1], near(X, delta))
    h_local = pltpu.make_async_copy(sh_hbm.at[seg(x, SEGR)], hid.at[c, x], loc.at[1])
    h_local.start()

    def block(ref, g, p, q, h):
        width, order = GROUPS[g]
        at = list(mine)
        for axis in order[:p]:
            at[axis] = pl.ds(0, RING)
        at[order[p]] = q
        return ref.at[at[0], at[1], at[2], :, pl.ds(h * (width // 2), width // 2)]

    def ag_copy(g, p, d, k, q, h):
        ref = block(w[g], g, p, q, h)
        return remote(ref, ref, ag_s.at[g, p, d, k], ag_r.at[g, p, d, k], near(GROUPS[g][1][p], 1 - 2 * d))

    def ag_start(g, p):
        m = mine[GROUPS[g][1][p]]
        for k in range(2):
            for d in range(2):
                copy = ag_copy(g, p, d, k, m, k ^ d)
                copy.start()
                sent.append(copy)

    def ag_forward(g, p):
        m = mine[GROUPS[g][1][p]]
        for d in range(2):
            ag_copy(g, p, d, 0, wrap(m - 1 + 2 * d), d).wait_recv()
            copy = ag_copy(g, p, d, 2, wrap(m - 1 + 2 * d), d)
            copy.start()
            sent.append(copy)

    def ag_finish(g, p):
        m = mine[GROUPS[g][1][p]]
        for d in range(2):
            ag_copy(g, p, d, 1, wrap(m - 1 + 2 * d), 1 - d).wait_recv()
            ag_copy(g, p, d, 2, wrap(m + 2), d).wait_recv()

    w_local.wait()
    remote(mw_hbm.at[0, :, cols(c)], wbuf.at[oc], ms.at[0], mr.at[0], other).wait_recv()
    for g, (width, _) in enumerate(GROUPS):
        rows = wbuf[:, :, OFFSETS[g] : OFFSETS[g] + width].reshape(ROWS, width)
        w[g][x, z, y] = rows.astype(BF16)
    for g in range(NG):
        ag_start(g, 0)

    og_local = pltpu.make_async_copy(og_hbm.at[:, :, cols(c)], og.at[c], loc.at[2])
    og_local.start()
    push(og_hbm.at[:, :, cols(oc)], og.at[c], ms.at[2], mr.at[2], other)
    push(sh_hbm.at[seg(x, SEGR)], hid.at[c, x], hcs.at[0], hcr.at[0], other)

    for g in range(NG):
        ag_forward(g, 0)
    for g in range(NG):
        ag_finish(g, 0)
    for g in range(NG):
        ag_start(g, 1)

    for d, delta in enumerate((1, -1)):
        remote(fwd.at[d], fwd.at[d], hs.at[d, 0], hr.at[d, 0], near(X, delta)).wait_recv()
        push(
            fwd.at[d],
            hid.at[c, wrap(x - delta), pl.ds(d * HS, HS)],
            hs.at[d, 2],
            hr.at[d, 2],
            near(X, delta),
        )

    for g in range(NG):
        ag_forward(g, 1)
    for g in range(NG):
        ag_finish(g, 1)
    for g in range(NG):
        ag_start(g, 2)

    remote(tgt.at[oc], tgt.at[oc], ms.at[1], mr.at[1], other).wait_recv()
    t_smem = pltpu.make_async_copy(tgt, tsm, loc.at[3])
    t_smem.start()
    t_smem.wait()

    def weight_grad(t):
        slots = []
        for k in range(2):
            count = jnp.int32(0)
            index = [jnp.int32(0)] * CAP
            valid = [jnp.int32(0)] * CAP
            for b in range(BLOCKS):
                hit = (tsm[k, b, 0] == t).astype(jnp.int32)
                for r in range(CAP):
                    here = hit * (count == r).astype(jnp.int32)
                    index[r] = index[r] + b * here
                    valid[r] = valid[r] + here
                count = count + hit
            for r in range(CAP):
                slots.append((k, index[r]))
                rows = hid[k, t, r * BLOCK : (r + 1) * BLOCK, :].astype(F32) * valid[r].astype(F32)
                at = (k * CAP + r) * BLOCK
                hid_t[:, at : at + BLOCK] = rows.astype(BF16).T
        for g, (width, _) in enumerate(GROUPS):

            def tile(j, carry, g=g):
                start = pl.multiple_of(j * TILE, TILE)
                rhs = jnp.concatenate(
                    [og[k, i, :, pl.ds(OFFSETS[g] + start, TILE)] for k, i in slots], axis=0
                )
                out = jnp.dot(hid_t[...], rhs, preferred_element_type=F32)
                part[g][t, :, :, :, pl.ds(start, TILE)] = out.astype(BF16).reshape(RING, RING, ROWS, TILE)
                return carry

            lax.fori_loop(0, width // TILE, tile, 0)

    def hid_peer(k, t):
        remote(hid.at[oc, t], hid.at[oc, t], hcs.at[k], hcr.at[k], other).wait_recv()

    h_local.wait()
    og_local.wait()
    remote(og_hbm.at[:, :, cols(c)], og.at[oc], ms.at[2], mr.at[2], other).wait_recv()
    hid_peer(0, x)
    weight_grad(x)
    for k, d, delta in ((1, 1, 1), (3, 0, -1)):
        t = wrap(x + delta)
        remote(hid.at[c, t], hid.at[c, t], hs.at[d, 1], hr.at[d, 1], near(X, -delta)).wait_recv()
        push(hid.at[c, t], hid.at[c, t], hcs.at[k], hcr.at[k], other)
    for k, delta in ((1, 1), (3, -1)):
        t = wrap(x + delta)
        hid_peer(k, t)
        weight_grad(t)
    for g in range(NG):
        ag_forward(g, 2)
    t = wrap(x + 2)
    for d, delta in enumerate((1, -1)):
        ref = hid.at[c, t, pl.ds(d * HS, HS)]
        remote(ref, ref, hs.at[d, 2], hr.at[d, 2], near(X, delta)).wait_recv()
    push(hid.at[c, t], hid.at[c, t], hcs.at[2], hcr.at[2], other)
    hid_peer(2, t)
    weight_grad(t)

    def rs_copy(g, p, d, k, q, h):
        return remote(
            block(part[g], g, p, q, h),
            land[g][p].at[d, k],
            rs_s.at[g, p, d, k],
            rs_r.at[g, p, d, k],
            near(GROUPS[g][1][p], 1 - 2 * d),
        )

    def rs_send(*a):
        copy = rs_copy(*a)
        copy.start()
        sent.append(copy)

    def rs_start(g, p):
        m = mine[GROUPS[g][1][p]]
        for d in range(2):
            rs_send(g, p, d, 0, wrap(m + 2), d)
        for d in range(2):
            rs_send(g, p, d, 1, wrap(m + 1 - 2 * d), 1 - d)

    def add_in(g, p, q, h, parts):
        width, order = GROUPS[g]
        half = width // 2
        free = sorted(order[:p])
        span = pl.ds(h * half, half)

        def one(i, carry):
            lead = (i // RING, lax.rem(i, RING)) if p == 2 else ((i,) if p == 1 else ())
            at = list(mine)
            for axis, v in zip(free, lead):
                at[axis] = v
            at[order[p]] = q
            total = part[g][at[0], at[1], at[2], :, span].astype(F32)
            for d, k in parts:
                total = total + land[g][p][(d, k) + lead].astype(F32)
            if p == 0 and len(parts) == 2:
                fin[:, OFFSETS[g] + h * half : OFFSETS[g] + (h + 1) * half] = total
            else:
                part[g][at[0], at[1], at[2], :, span] = total.astype(BF16)
            return carry

        if p == 0:
            one(0, 0)
        else:
            lax.fori_loop(0, RING**p, one, 0)

    def rs_middle(g, p):
        m = mine[GROUPS[g][1][p]]
        for d in range(2):
            q = wrap(m + 1 - 2 * d)
            rs_copy(g, p, d, 0, q, d).wait_recv()
            add_in(g, p, q, d, ((d, 0),))
            rs_send(g, p, d, 2, q, d)

    def rs_finish(g, p):
        m = mine[GROUPS[g][1][p]]
        for k in (1, 2):
            for d in range(2):
                rs_copy(g, p, d, k, m, d if k == 2 else 1 - d).wait_recv()
        add_in(g, p, m, 0, ((0, 2), (1, 1)))
        add_in(g, p, m, 1, ((0, 1), (1, 2)))

    for g in range(NG):
        rs_start(g, 2)

    for g in range(NG):
        ag_finish(g, 2)

    def half_product(k, b):
        t = tsm[k, b, 0]
        acc = jnp.zeros((BLOCK, FF), F32)
        for g, (width, _) in enumerate(GROUPS):
            lhs = og[k, b, :, OFFSETS[g] : OFFSETS[g] + width]
            rhs = w[g][t].reshape(FF, width)
            acc = acc + lax.dot_general(lhs, rhs, (((1,), (1,)), ((), ())), preferred_element_type=F32)
        return acc

    def for_peer(b, carry):
        hsend[b] = half_product(oc, b).astype(BF16)
        remote(hsend.at[b], hrecv.at[b], hps.at[b], hpr.at[b], other).start()
        return carry

    lax.fori_loop(0, BLOCKS, for_peer, 0)
    for g in range(NG):
        rs_middle(g, 2)

    def for_me(b, carry):
        acc = half_product(c, b)
        remote(hsend.at[b], hrecv.at[b], hps.at[b], hpr.at[b], other).wait_recv()
        hrecv[b] = ((acc + hrecv[b].astype(F32)) * (D**-0.5)).astype(BF16)
        pltpu.make_async_copy(hrecv.at[b], hg_hbm.at[b], hos.at[b]).start()
        return carry

    lax.fori_loop(0, BLOCKS, for_me, 0)
    for g in range(NG):
        rs_finish(g, 2)
    for p in (1, 0):
        for g in range(NG):
            rs_start(g, p)
        for g in range(NG):
            rs_middle(g, p)
        for g in range(NG):
            rs_finish(g, p)

    def rows_of(who):
        return pl.ds(pl.multiple_of(who * (ROWS // 2), 8), ROWS // 2)

    push(fin.at[rows_of(oc)], wgs.at[:, cols(c)], ms.at[3], mr.at[3], other)
    wgs[:, cols(c)] = fin[rows_of(c), :]
    remote(fin.at[rows_of(c)], wgs.at[:, cols(oc)], ms.at[3], mr.at[3], other).wait_recv()
    wg_ref[...] = wgs[...]

    def drain(b, carry):
        remote(hsend.at[b], hrecv.at[b], hps.at[b], hpr.at[b], other).wait_send()
        pltpu.make_async_copy(hrecv.at[b], hg_hbm.at[b], hos.at[b]).wait()
        return carry

    lax.fori_loop(0, BLOCKS, drain, 0)
    for copy in sent:
        copy.wait_send()


def exchange(out_grad, block_target, saved_hidden, master_weight):
    scratch = [pltpu.VMEM((2, BLOCKS, BLOCK, HALF), BF16)]
    for _ in range(2):
        scratch += [pltpu.VMEM((RING, RING, RING, ROWS, width), BF16) for width, _ in GROUPS]
    for width, _ in GROUPS:
        scratch += [pltpu.VMEM((2, 3) + (RING,) * p + (ROWS, width // 2), BF16) for p in range(3)]
    dma = pltpu.SemaphoreType.DMA
    scratch += [
        pltpu.VMEM((2, EXPERTS, CAP * BLOCK, FF), BF16),
        pltpu.VMEM((2, CAP * BLOCK // 2, FF), BF16),
        pltpu.VMEM((FF, 2 * CAP * BLOCK), BF16),
        pltpu.VMEM((2, ROWS // 2, HALF), F32),
        pltpu.VMEM((2, BLOCKS, 128), jnp.int32),
        pltpu.SMEM((2, BLOCKS, 128), jnp.int32),
        pltpu.VMEM((BLOCKS, BLOCK, FF), BF16),
        pltpu.VMEM((BLOCKS, BLOCK, FF), BF16),
        pltpu.VMEM((ROWS, HALF), F32),
        pltpu.VMEM((ROWS // 2, D), F32),
        dma((NG, 3, 2, 3)),
        dma((NG, 3, 2, 3)),
        dma((NG, 3, 2, 3)),
        dma((NG, 3, 2, 3)),
        dma((2, 3)),
        dma((2, 3)),
        dma((4,)),
        dma((4,)),
        dma((4,)),
        dma((4,)),
        dma((4,)),
        dma((BLOCKS,)),
        dma((BLOCKS,)),
        dma((BLOCKS,)),
    ]
    anywhere = pl.BlockSpec(memory_space=pl.ANY)
    return pl.pallas_call(
        kernel,
        out_shape=(
            jax.ShapeDtypeStruct((BLOCKS, BLOCK, FF), BF16),
            jax.ShapeDtypeStruct((ROWS // 2, D), F32),
        ),
        in_specs=[anywhere, pl.BlockSpec(memory_space=pltpu.VMEM), anywhere, anywhere],
        out_specs=(anywhere, pl.BlockSpec(memory_space=pltpu.VMEM)),
        scratch_shapes=scratch,
        compiler_params=pltpu.CompilerParams(
            collective_id=0, has_side_effects=True, vmem_limit_bytes=63 * 1024 * 1024
        ),
        cost_estimate=pl.CostEstimate(flops=20 * 10**9, bytes_accessed=16 * 2**20, transcendentals=0),
    )(out_grad.reshape(BLOCKS, BLOCK, D), block_target, saved_hidden, master_weight)


def body(out_grad, block_target, saved_hidden, master_weight, first_moment, second_moment):
    hidden, total = exchange(out_grad, block_target, saved_hidden, master_weight)
    hidden_grad = hidden.reshape(BLOCKS * BLOCK, FF)
    weight_grad = total[None] * (D**-0.5)
    new_first = BETA_ONE * first_moment + (1.0 - BETA_ONE) * weight_grad
    new_second = BETA_TWO * second_moment + (1.0 - BETA_TWO) * weight_grad * weight_grad
    first_fix = 1.0 - BETA_ONE**STEP
    second_fix = 1.0 - BETA_TWO**STEP
    new_weight = master_weight - LEARN_RATE * (new_first / first_fix) / (
        jnp.sqrt(new_second / second_fix) + EPSILON
    )
    return (hidden_grad, new_weight, new_first, new_second)


def solution(mesh):
    rows = P(("ep", "edp"), None)
    shard = P("ep", "edp", None)
    return jax.shard_map(
        body,
        mesh=mesh,
        in_specs=(rows, rows, rows, shard, shard, shard),
        out_specs=(rows, shard, shard, shard),
        check_vma=False,
    )
```

time: 479 us -> 170 us (0.35)
  blocking collectives: 228 us -> 0 us
  Pallas kernels: 0 us -> 164 us
  waiting for transfers between devices: 138 us -> 0 us
  matrix products: 49.1 us -> 0 us
  local copies, waits for them, and re-layouts: 44.6 us -> 2.48 us
  between operations: 14.1 us -> 0.66 us
    all_to_all x2 -> x0, blocking collectives: 228 us -> none  [the longest x1 187 us: body(): lax.all_to_all(outbound, 'ep', split_axis=0, concat_axis=0, tiled=True)]
    pallas_call x0 -> x1, Pallas kernels: none -> 164 us  [exchange(): pl.pallas_call(kernel, out_shape=(jax.ShapeDtypeStruct((BLOCKS, BLOCK, FF...]
    reduce_scatter x1 -> x0, waiting for transfers between devices: 86.6 us -> none  [body(): lax.psum_scatter(grad_term.astype(jnp.bfloat16), 'edp', scatter_dimension...]
    all_gather x1 -> x0, waiting for transfers between devices: 51.5 us -> none  [body(): lax.all_gather(weight_low, 'edp', axis=1, tiled=True)[0]]
    dot_general x4 -> x0, matrix products: 49.1 us -> none  [the longest x1 18.2 us: body(): lax.dot_general(flat_rows, lax.all_gather(weight_low, 'edp', axis=1, tile...]
    unnamed x15 -> x8, local copies, waits for them, and re-layouts: 31 us -> 2.48 us
    reshape x2 -> x0, local copies, waits for them, and re-layouts: 13.6 us -> none  [the longest x1 10.4 us: body(): grad_blocks = out_grad.reshape(blocks, BLOCK * model_width)]
  transfers between devices with their start and end apart: 2 -> 0, of which waited for: 2 -> 0; matrix products, arithmetic and copies ran while one was open for 0% -> 0% of each run, Pallas kernels for 0% -> 0%
where the time goes in v1:
time: 170 us
  Pallas kernels  164 us (96%)
  local copies, waits for them, and re-layouts  2.48 us (1%)
  other arithmetic  2.39 us (1%)
    pallas_call x1, Pallas kernels, exchange(): pl.pallas_call(kernel, out_shape=(jax.ShapeDtypeStruct((BLOCKS, BLOCK, FF...  164 us

profile of v1, /device:TPU:1, one launch (start us, length us, event | category | flops | bytes accessed | tf_op | source)
XLA Modules:
  0.0 169.8 jit_solution(13842593167180400368)
XLA Ops:
  0.6 1.3 copy.10.bt_ref
  2.0 0.0 copy-start.1
  2.0 0.0 copy-start.2
  2.0 164.3 %shard_map.93 = (bf16[8,128,768]{2,1,0:T(8,128)(2,1)}, f32[24,4096]{1,0:T(8,128)}) custom-call(bf16[8,128,4096]{2,1,0:T(8,128)(2,1)} %bitcast.9, s32[8,1]{1,0:T(8,128)} %copy.10.bt_ref, bf16[2048,768]{1,0:T(8,128)(2,1)} %sh_hbm.1, f32[1,24,4096]{2,1,0:T(8,128)} %mw_hbm.1), custom_call_target="tpu_custom_call" | custom-call | flops 20000000000 | bytes 16777216 | tf_op jit(solution)/shard_map/pallas_call | solution.py:404
  166.2 0.0 copy-start
  166.2 0.0 copy-done.1
  166.2 0.0 copy-done.2
  166.3 2.4 %divide_subtract_fusion = (f32[1,24,4096]{2,1,0:T(8,128)}, f32[1,24,4096]{2,1,0:T(8,128)}, f32[1,24,4096]{2,1,0:T(8,128)}) fusion(f32[1,24,4096]{2,1,0:T(8,128)S(1)} %copy-done.1, f32[24,4096]{1,0:T(8,128)} %get-tuple-element.7, f32[1,24,4096]{2,1,0:T(8,128)S(1)} %copy-done.2, f32[1,24,4096]{2,1,0:T(8,128)} %param.11), kind=kLoop, calls=%fused_computation.2 | loop fusion | flops 1277952 | bytes 2752512 | tf_op jit(solution)/shard_map/sub | solution.py:428
  168.6 0.0 copy-done
  168.6 1.1 copy.12
Async XLA Ops:
  2.0 164.3 %copy-start.1 = (f32[1,24,4096]{2,1,0:T(8,128)S(1)}, f32[1,24,4096]{2,1,0:T(8,128)}, u32[]{:S(2)}) copy-start(f32[1,24,4096]{2,1,0:T(8,128)} %mw_hbm.1) | copy-start | bytes 1179652
  2.0 164.3 %copy-start.2 = (f32[1,24,4096]{2,1,0:T(8,128)S(1)}, f32[1,24,4096]{2,1,0:T(8,128)}, u32[]{:S(2)}) copy-start(f32[1,24,4096]{2,1,0:T(8,128)} %param.10) | copy-start | bytes 1179652
  166.2 2.4 %copy-start = (bf16[8,128,768]{2,1,0:T(8,128)(2,1)S(1)}, bf16[8,128,768]{2,1,0:T(8,128)(2,1)}, u32[]{:S(2)}) copy-start(bf16[8,128,768]{2,1,0:T(8,128)(2,1)} %get-tuple-element.6) | copy-start | bytes 4718596

commit v2 on v1

v2 whole, which is shorter than its diff:
```python
import jax
import jax.numpy as jnp
from jax import lax
from jax.experimental import pallas as pl
from jax.experimental.pallas import tpu as pltpu
from jax.sharding import PartitionSpec as P

MESH = pl.DeviceIdType.MESH
F32 = jnp.float32
BF16 = jnp.bfloat16

BLOCK = 128
STEP = 1000
BETA_ONE = 0.9
BETA_TWO = 0.999
LEARN_RATE = 0.01
EPSILON = 1e-08

RING = 4
EXPERTS = 4
CAP = 4
BLOCKS = 8
D = 4096
HALF = D // 2
FF = 768
ROWS = 48
X, Z, Y = 0, 1, 2
GROUPS = ((256, (X, Z, Y)), (256, (X, Y, Z)), (512, (X, Z, Y)), (512, (X, Y, Z)), (512, (Y, Z, X)))
OFFSETS = (0, 256, 512, 1024, 1536)
NG = len(GROUPS)
TILE = 256
UNIT = 4

ORDER = (
    ("as", 0, 0), ("as", 1, 0), ("as", 2, 0), ("as", 3, 0), ("as", 4, 0), ("a2a",), ("as", 0, 1), ("as", 1, 1),
    ("as", 4, 1), ("af", 0, 1), ("as", 2, 1), ("af", 1, 1), ("as", 3, 1), ("af", 4, 1), ("ht", 0), ("as", 1, 2),
    ("wg", 0, 0), ("wg", 0, 1), ("wg", 0, 2), ("as", 0, 2), ("af", 3, 1), ("wg", 0, 3), ("wg", 0, 4), ("af", 2, 1),
    ("as", 4, 2), ("af", 0, 2), ("af", 1, 2), ("as", 3, 2), ("hp", 1), ("hp", 3), ("ht", 1), ("as", 2, 2),
    ("ae", 0, 2), ("wg", 1, 0), ("wg", 1, 1), ("wg", 1, 2), ("wg", 1, 3), ("wg", 1, 4), ("ae", 1, 2), ("ht", 3),
    ("wg", 3, 0), ("wg", 3, 1), ("wg", 3, 2), ("wg", 3, 3), ("wg", 3, 4), ("af", 2, 2), ("af", 3, 2), ("hp", 2),
    ("ht", 2), ("wg", 2, 0), ("rs", 0, 2), ("wg", 2, 1), ("rs", 1, 2), ("wg", 2, 2), ("rs", 2, 2), ("wg", 2, 3),
    ("rs", 3, 2), ("wg", 2, 4), ("af", 4, 2), ("rs", 4, 2), ("ae", 2, 2), ("ae", 3, 2), ("rm", 0, 2), ("rm", 1, 2),
    ("ae", 4, 2), ("hg", 0), ("hg", 1), ("rm", 2, 2), ("rm", 3, 2), ("rm", 4, 2), ("hg", 2), ("hg", 3), ("rs", 0, 1),
    ("rs", 1, 1), ("rs", 4, 1), ("rm", 1, 1), ("rs", 2, 1), ("rm", 0, 1), ("rs", 1, 0), ("rs", 3, 1), ("rm", 2, 1),
    ("rm", 4, 1), ("re", 1, 0), ("rs", 0, 0), ("rm", 3, 1), ("rs", 2, 0), ("re", 0, 0), ("rs", 4, 0), ("rs", 3, 0),
    ("re", 2, 0), ("re", 4, 0), ("re", 3, 0),
)


def kernel(og_hbm, bt_hbm, sh_hbm, mw_hbm, hg_hbm, wg_ref, *scratch):
    it = iter(scratch)
    bt_ref = next(it)
    og = next(it)
    w = [next(it) for _ in range(NG)]
    part = [next(it) for _ in range(NG)]
    land = [[next(it) for _ in range(3)] for _ in range(NG)]
    hid = next(it)
    hid_t = next(it)
    wbuf = next(it)
    tgt = next(it)
    tsm = next(it)
    hsend = next(it)
    hrecv = next(it)
    fin = next(it)
    wgs = next(it)
    ag_s, ag_r, rs_s, rs_r = next(it), next(it), next(it), next(it)
    hs, hr, hcs, hcr = next(it), next(it), next(it), next(it)
    ms, mr = next(it), next(it)
    loc = next(it)
    hps, hpr, hos = next(it), next(it), next(it)

    x = lax.axis_index("ep")
    e = lax.axis_index("edp")
    c = lax.rem(e, 2)
    y = lax.rem(e // 2, RING)
    z = e // (2 * RING)
    oc = 1 - c
    mine = (x, z, y)

    def wrap(v):
        return lax.rem(v + RING, RING)

    def near(axis, delta):
        at = list(mine)
        at[axis] = wrap(at[axis] + delta)
        return (at[0], (at[1] * RING + at[2]) * 2 + c)

    other = (x, e + 1 - 2 * c)

    barrier = pltpu.get_barrier_semaphore()
    peers = [near(axis, delta) for axis in (X, Z, Y) for delta in (1, -1)]
    peers += [near(axis, 2) for axis in sorted({X} | {order[0] for _, order in GROUPS})] + [other]
    for peer in peers:
        pl.semaphore_signal(barrier, inc=1, device_id=peer, device_id_type=MESH)
    bt_local = pltpu.make_async_copy(bt_hbm, bt_ref, loc.at[4])
    bt_local.start()
    pl.semaphore_wait(barrier, len(peers))

    sent = []

    def remote(src, dst, s, r, dev):
        return pltpu.make_async_remote_copy(
            src_ref=src, dst_ref=dst, send_sem=s, recv_sem=r, device_id=dev, device_id_type=MESH
        )

    def push(*a):
        copy = remote(*a)
        copy.start()
        sent.append(copy)
        return copy

    def cols(who):
        return pl.ds(pl.multiple_of(who * HALF, HALF), HALF)

    def seg(who, n):
        return pl.ds(pl.multiple_of(who * CAP * BLOCK, CAP * BLOCK), n)

    SEGR = CAP * BLOCK
    w_local = pltpu.make_async_copy(mw_hbm.at[0, :, cols(c)], wbuf.at[c], loc.at[0])
    w_local.start()
    w_peer = push(mw_hbm.at[0, :, cols(oc)], wbuf.at[c], ms.at[0], mr.at[0], other)
    h_local = pltpu.make_async_copy(sh_hbm.at[seg(x, SEGR)], hid.at[c, x], loc.at[1])
    h_local.start()
    bt_local.wait()
    tgt[c] = jnp.broadcast_to(bt_ref[...], (BLOCKS, 128))
    push(tgt.at[c], tgt.at[c], ms.at[1], mr.at[1], other)

    def a2a():
        for i, delta in enumerate((1, -1, 2)):
            push(sh_hbm.at[seg(wrap(x + delta), SEGR)], hid.at[c, x], hs.at[i], hr.at[i], near(X, delta))

    def hid_push(k):
        t = wrap(x + k)
        i = (None, 1, 2, 0)[k]
        remote(hid.at[c, t], hid.at[c, t], hs.at[i], hr.at[i], near(X, k)).wait_recv()
        push(hid.at[c, t], hid.at[c, t], hcs.at[k], hcr.at[k], other)

    def block(ref, g, p, q, h):
        width, order = GROUPS[g]
        at = list(mine)
        for axis in order[:p]:
            at[axis] = pl.ds(0, RING)
        at[order[p]] = q
        if h is None:
            return ref.at[at[0], at[1], at[2]]
        return ref.at[at[0], at[1], at[2], :, pl.ds(h * (width // 2), width // 2)]

    def ag_copy(g, p, d, k, q, h):
        ref = block(w[g], g, p, q, h)
        return remote(ref, ref, ag_s.at[g, p, d, k], ag_r.at[g, p, d, k], near(GROUPS[g][1][p], 1 - 2 * d))

    DELTAS = (1, -1, 2)

    def ag_direct(g, k, q):
        ref = block(w[g], g, 0, q, None)
        return remote(ref, ref, ag_s.at[g, 0, 0, k], ag_r.at[g, 0, 0, k], near(GROUPS[g][1][0], DELTAS[k]))

    def ag_start(g, p):
        m = mine[GROUPS[g][1][p]]
        if p == 0:
            for k in range(3):
                copy = ag_direct(g, k, m)
                copy.start()
                sent.append(copy)
            return
        ag_finish(g, p - 1)
        for k in range(2):
            for d in range(2):
                copy = ag_copy(g, p, d, k, m, k ^ d)
                copy.start()
                sent.append(copy)

    def ag_forward(g, p):
        m = mine[GROUPS[g][1][p]]
        for d in range(2):
            ag_copy(g, p, d, 0, wrap(m - 1 + 2 * d), d).wait_recv()
            copy = ag_copy(g, p, d, 2, wrap(m - 1 + 2 * d), d)
            copy.start()
            sent.append(copy)

    def ag_finish(g, p):
        m = mine[GROUPS[g][1][p]]
        if p == 0:
            for k in range(3):
                ag_direct(g, k, wrap(m - DELTAS[k])).wait_recv()
            return
        for d in range(2):
            ag_copy(g, p, d, 1, wrap(m - 1 + 2 * d), 1 - d).wait_recv()
            ag_copy(g, p, d, 2, wrap(m + 2), d).wait_recv()

    w_local.wait()
    remote(mw_hbm.at[0, :, cols(c)], wbuf.at[oc], ms.at[0], mr.at[0], other).wait_recv()
    for g, (width, _) in enumerate(GROUPS):
        rows = wbuf[:, :, OFFSETS[g] : OFFSETS[g] + width].reshape(ROWS, width)
        w[g][x, z, y] = rows.astype(BF16)

    og_local = pltpu.make_async_copy(og_hbm.at[:, :, cols(c)], og.at[c], loc.at[2])
    og_local.start()
    push(og_hbm.at[:, :, cols(oc)], og.at[c], ms.at[2], mr.at[2], other)
    push(sh_hbm.at[seg(x, SEGR)], hid.at[c, x], hcs.at[0], hcr.at[0], other)

    slots = {}

    def take(k):
        t = wrap(x + k)
        if k == 0:
            remote(tgt.at[oc], tgt.at[oc], ms.at[1], mr.at[1], other).wait_recv()
            t_smem = pltpu.make_async_copy(tgt, tsm, loc.at[3])
            t_smem.start()
            t_smem.wait()
            h_local.wait()
            og_local.wait()
            remote(og_hbm.at[:, :, cols(c)], og.at[oc], ms.at[2], mr.at[2], other).wait_recv()
        remote(hid.at[oc, t], hid.at[oc, t], hcs.at[k], hcr.at[k], other).wait_recv()
        slots[k] = []
        for core in range(2):
            count = jnp.int32(0)
            index = [jnp.int32(0)] * CAP
            valid = [jnp.int32(0)] * CAP
            for b in range(BLOCKS):
                hit = (tsm[core, b, 0] == t).astype(jnp.int32)
                for r in range(CAP):
                    here = hit * (count == r).astype(jnp.int32)
                    index[r] = index[r] + b * here
                    valid[r] = valid[r] + here
                count = count + hit
            for r in range(CAP):
                slots[k].append((core, index[r]))
                rows = hid[core, t, r * BLOCK : (r + 1) * BLOCK, :].astype(F32) * valid[r].astype(F32)
                at = (core * CAP + r) * BLOCK
                hid_t[:, at : at + BLOCK] = rows.astype(BF16).T

    def weight_grad(k, g):
        t = wrap(x + k)
        width = GROUPS[g][0]

        def tile(j, carry):
            start = pl.multiple_of(j * TILE, TILE)
            rhs = jnp.concatenate(
                [og[core, i, :, pl.ds(OFFSETS[g] + start, TILE)] for core, i in slots[k]], axis=0
            )
            out = jnp.dot(hid_t[...], rhs, preferred_element_type=F32)
            part[g][t, :, :, :, pl.ds(start, TILE)] = out.astype(BF16).reshape(RING, RING, ROWS, TILE)
            return carry

        lax.fori_loop(0, width // TILE, tile, 0)

    def rs_copy(g, p, d, k, q, h):
        return remote(
            block(part[g], g, p, q, h),
            land[g][p].at[d, k],
            rs_s.at[g, p, d, k],
            rs_r.at[g, p, d, k],
            near(GROUPS[g][1][p], 1 - 2 * d),
        )

    def rs_send(*a):
        copy = rs_copy(*a)
        copy.start()
        sent.append(copy)

    def rs_direct(g, k, q):
        return remote(
            block(part[g], g, 0, q, None),
            land[g][0].at[k],
            rs_s.at[g, 0, 0, k],
            rs_r.at[g, 0, 0, k],
            near(GROUPS[g][1][0], DELTAS[k]),
        )

    def rs_start(g, p):
        m = mine[GROUPS[g][1][p]]
        if p < 2:
            rs_finish(g, p + 1)
        if p == 0:
            for k in range(3):
                copy = rs_direct(g, k, wrap(m + DELTAS[k]))
                copy.start()
                sent.append(copy)
            return
        for d in range(2):
            rs_send(g, p, d, 0, wrap(m + 2), d)
        for d in range(2):
            rs_send(g, p, d, 1, wrap(m + 1 - 2 * d), 1 - d)

    def add_in(g, p, q, h, parts):
        width, order = GROUPS[g]
        half = width // 2
        free = sorted(order[:p])
        span = pl.ds(h * half, half)

        def one(i, carry):
            lead = (i // RING, lax.rem(i, RING)) if p == 2 else (i,)
            at = list(mine)
            for axis, v in zip(free, lead):
                at[axis] = v
            at[order[p]] = q
            total = part[g][at[0], at[1], at[2], :, span].astype(F32)
            for d, k in parts:
                total = total + land[g][p][(d, k) + lead].astype(F32)
            part[g][at[0], at[1], at[2], :, span] = total.astype(BF16)
            return carry

        lax.fori_loop(0, RING**p, one, 0)

    def rs_middle(g, p):
        m = mine[GROUPS[g][1][p]]
        for d in range(2):
            q = wrap(m + 1 - 2 * d)
            rs_copy(g, p, d, 0, q, d).wait_recv()
            add_in(g, p, q, d, ((d, 0),))
            rs_send(g, p, d, 2, q, d)

    def rs_finish(g, p):
        m = mine[GROUPS[g][1][p]]
        if p == 0:
            total = part[g][mine].astype(F32)
            for k in range(3):
                rs_direct(g, k, m).wait_recv()
                total = total + land[g][0][k].astype(F32)
            fin[:, OFFSETS[g] : OFFSETS[g] + GROUPS[g][0]] = total
            return
        for k in (1, 2):
            for d in range(2):
                rs_copy(g, p, d, k, m, d if k == 2 else 1 - d).wait_recv()
        add_in(g, p, m, 0, ((0, 2), (1, 1)))
        add_in(g, p, m, 1, ((0, 1), (1, 2)))

    def half_product(k, b):
        t = tsm[k, b, 0]
        acc = jnp.zeros((BLOCK, FF), F32)
        for g, (width, _) in enumerate(GROUPS):
            lhs = og[k, b, :, OFFSETS[g] : OFFSETS[g] + width]
            rhs = w[g][t].reshape(FF, width)
            acc = acc + lax.dot_general(lhs, rhs, (((1,), (1,)), ((), ())), preferred_element_type=F32)
        return acc

    def for_peer(b, carry):
        hsend[b] = half_product(oc, b).astype(BF16)
        remote(hsend.at[b], hrecv.at[b], hps.at[b], hpr.at[b], other).start()
        return carry

    def for_me(b, carry):
        acc = half_product(c, b)
        remote(hsend.at[b], hrecv.at[b], hps.at[b], hpr.at[b], other).wait_recv()
        hrecv[b] = ((acc + hrecv[b].astype(F32)) * (D**-0.5)).astype(BF16)
        pltpu.make_async_copy(hrecv.at[b], hg_hbm.at[b], hos.at[b]).start()
        return carry

    def hidden_grad(u):
        start = u * UNIT
        if start < BLOCKS:
            lax.fori_loop(start, start + UNIT, for_peer, 0)
        else:
            lax.fori_loop(start - BLOCKS, start - BLOCKS + UNIT, for_me, 0)

    steps = {
        "as": ag_start,
        "af": ag_forward,
        "ae": ag_finish,
        "a2a": a2a,
        "hp": hid_push,
        "ht": take,
        "wg": weight_grad,
        "rs": rs_start,
        "rm": rs_middle,
        "re": rs_finish,
        "hg": hidden_grad,
    }
    for name, *where in ORDER:
        steps[name](*where)

    def rows_of(who):
        return pl.ds(pl.multiple_of(who * (ROWS // 2), 8), ROWS // 2)

    push(fin.at[rows_of(oc)], wgs.at[:, cols(c)], ms.at[3], mr.at[3], other)
    wgs[:, cols(c)] = fin[rows_of(c), :]
    remote(fin.at[rows_of(c)], wgs.at[:, cols(oc)], ms.at[3], mr.at[3], other).wait_recv()
    wg_ref[...] = wgs[...]

    def drain(b, carry):
        remote(hsend.at[b], hrecv.at[b], hps.at[b], hpr.at[b], other).wait_send()
        pltpu.make_async_copy(hrecv.at[b], hg_hbm.at[b], hos.at[b]).wait()
        return carry

    lax.fori_loop(0, BLOCKS, drain, 0)
    for copy in sent:
        copy.wait_send()


def exchange(out_grad, block_target, saved_hidden, master_weight):
    scratch = [pltpu.VMEM((BLOCKS, 1), jnp.int32), pltpu.VMEM((2, BLOCKS, BLOCK, HALF), BF16)]
    for _ in range(2):
        scratch += [pltpu.VMEM((RING, RING, RING, ROWS, width), BF16) for width, _ in GROUPS]
    for width, _ in GROUPS:
        scratch += [pltpu.VMEM((3, ROWS, width), BF16)]
        scratch += [pltpu.VMEM((2, 3) + (RING,) * p + (ROWS, width // 2), BF16) for p in (1, 2)]
    dma = pltpu.SemaphoreType.DMA
    scratch += [
        pltpu.VMEM((2, EXPERTS, CAP * BLOCK, FF), BF16),
        pltpu.VMEM((FF, 2 * CAP * BLOCK), BF16),
        pltpu.VMEM((2, ROWS // 2, HALF), F32),
        pltpu.VMEM((2, BLOCKS, 128), jnp.int32),
        pltpu.SMEM((2, BLOCKS, 128), jnp.int32),
        pltpu.VMEM((BLOCKS, BLOCK, FF), BF16),
        pltpu.VMEM((BLOCKS, BLOCK, FF), BF16),
        pltpu.VMEM((ROWS, HALF), F32),
        pltpu.VMEM((ROWS // 2, D), F32),
        dma((NG, 3, 2, 3)),
        dma((NG, 3, 2, 3)),
        dma((NG, 3, 2, 3)),
        dma((NG, 3, 2, 3)),
        dma((3,)),
        dma((3,)),
        dma((4,)),
        dma((4,)),
        dma((4,)),
        dma((4,)),
        dma((5,)),
        dma((BLOCKS,)),
        dma((BLOCKS,)),
        dma((BLOCKS,)),
    ]
    anywhere = pl.BlockSpec(memory_space=pl.ANY)
    return pl.pallas_call(
        kernel,
        out_shape=(
            jax.ShapeDtypeStruct((BLOCKS, BLOCK, FF), BF16),
            jax.ShapeDtypeStruct((ROWS // 2, D), F32),
        ),
        in_specs=[anywhere] * 4,
        out_specs=(anywhere, pl.BlockSpec(memory_space=pltpu.VMEM)),
        scratch_shapes=scratch,
        compiler_params=pltpu.CompilerParams(
            collective_id=0, has_side_effects=True, vmem_limit_bytes=63 * 1024 * 1024
        ),
        cost_estimate=pl.CostEstimate(flops=20 * 10**9, bytes_accessed=16 * 2**20, transcendentals=0),
    )(out_grad.reshape(BLOCKS, BLOCK, D), block_target, saved_hidden, master_weight)


def body(out_grad, block_target, saved_hidden, master_weight, first_moment, second_moment):
    hidden, total = exchange(out_grad, block_target, saved_hidden, master_weight)
    hidden_grad = hidden.reshape(BLOCKS * BLOCK, FF)
    weight_grad = total[None] * (D**-0.5)
    new_first = BETA_ONE * first_moment + (1.0 - BETA_ONE) * weight_grad
    new_second = BETA_TWO * second_moment + (1.0 - BETA_TWO) * weight_grad * weight_grad
    first_fix = 1.0 - BETA_ONE**STEP
    second_fix = 1.0 - BETA_TWO**STEP
    new_weight = master_weight - LEARN_RATE * (new_first / first_fix) / (
        jnp.sqrt(new_second / second_fix) + EPSILON
    )
    return (hidden_grad, new_weight, new_first, new_second)


def solution(mesh):
    rows = P(("ep", "edp"), None)
    shard = P("ep", "edp", None)
    return jax.shard_map(
        body,
        mesh=mesh,
        in_specs=(rows, rows, rows, shard, shard, shard),
        out_specs=(rows, shard, shard, shard),
        check_vma=False,
    )
```

time: 170 us -> 140 us (0.82)
  Pallas kernels: 164 us -> 135 us
    pallas_call x1, Pallas kernels: 164 us -> 135 us  [exchange(): pl.pallas_call(kernel, out_shape=(jax.ShapeDtypeStruct((BLOCKS, BLOCK, FF...]
where the time goes in v2:
time: 140 us
  Pallas kernels  135 us (96%)
  local copies, waits for them, and re-layouts  2.48 us (2%)
  other arithmetic  2.39 us (2%)
    pallas_call x1, Pallas kernels, exchange(): pl.pallas_call(kernel, out_shape=(jax.ShapeDtypeStruct((BLOCKS, BLOCK, FF...  135 us

profile of v2, /device:TPU:1, one launch (start us, length us, event | category | flops | bytes accessed | tf_op | source)
XLA Modules:
  0.0 140.1 jit_solution(6123159769544595322)
XLA Ops:
  0.6 1.3 copy.10.bt_hbm
  2.0 0.0 copy-start.1
  2.0 0.0 copy-start.2
  2.0 134.6 %shard_map.93 = (bf16[8,128,768]{2,1,0:T(8,128)(2,1)}, f32[24,4096]{1,0:T(8,128)}) custom-call(bf16[8,128,4096]{2,1,0:T(8,128)(2,1)} %bitcast.9, s32[8,1]{1,0:T(8,128)} %copy.10.bt_hbm, bf16[2048,768]{1,0:T(8,128)(2,1)} %sh_hbm.1, f32[1,24,4096]{2,1,0:T(8,128)} %mw_hbm.1), custom_call_target="tpu_custom_call" | custom-call | flops 20000000000 | bytes 16777216 | tf_op jit(solution)/shard_map/pallas_call | solution.py:425
  136.5 0.0 copy-start
  136.6 0.0 copy-done.1
  136.6 0.0 copy-done.2
  136.6 2.4 %divide_subtract_fusion = (f32[1,24,4096]{2,1,0:T(8,128)}, f32[1,24,4096]{2,1,0:T(8,128)}, f32[1,24,4096]{2,1,0:T(8,128)}) fusion(f32[1,24,4096]{2,1,0:T(8,128)S(1)} %copy-done.1, f32[24,4096]{1,0:T(8,128)} %get-tuple-element.7, f32[1,24,4096]{2,1,0:T(8,128)S(1)} %copy-done.2, f32[1,24,4096]{2,1,0:T(8,128)} %param.11), kind=kLoop, calls=%fused_computation.2 | loop fusion | flops 1277952 | bytes 2752512 | tf_op jit(solution)/shard_map/sub | solution.py:449
  139.0 0.0 copy-done
  139.0 1.1 copy.12
Async XLA Ops:
  2.0 134.6 %copy-start.1 = (f32[1,24,4096]{2,1,0:T(8,128)S(1)}, f32[1,24,4096]{2,1,0:T(8,128)}, u32[]{:S(2)}) copy-start(f32[1,24,4096]{2,1,0:T(8,128)} %mw_hbm.1) | copy-start | bytes 1179652
  2.0 134.6 %copy-start.2 = (f32[1,24,4096]{2,1,0:T(8,128)S(1)}, f32[1,24,4096]{2,1,0:T(8,128)}, u32[]{:S(2)}) copy-start(f32[1,24,4096]{2,1,0:T(8,128)} %param.10) | copy-start | bytes 1179652
  136.5 2.4 %copy-start = (bf16[8,128,768]{2,1,0:T(8,128)(2,1)S(1)}, bf16[8,128,768]{2,1,0:T(8,128)(2,1)}, u32[]{:S(2)}) copy-start(bf16[8,128,768]{2,1,0:T(8,128)(2,1)} %get-tuple-element.6) | copy-start | bytes 4718596

commit v3 on v2

--- a/solution.py
+++ b/solution.py
@@ -25,25 +25,36 @@
 FF = 768
 ROWS = 48
 X, Z, Y = 0, 1, 2
-GROUPS = ((256, (X, Z, Y)), (256, (X, Y, Z)), (512, (X, Z, Y)), (512, (X, Y, Z)), (512, (Y, Z, X)))
-OFFSETS = (0, 256, 512, 1024, 1536)
+GROUPS = (
+    (512, (X, Z, Y)),
+    (512, (X, Y, Z)),
+    (256, (X, Z, Y)),
+    (256, (Y, Z, X)),
+    (256, (X, Y, Z)),
+    (256, (Z, Y, X)),
+)
+OFFSETS = (0, 512, 1024, 1280, 1536, 1792)
+LATE = 1
 NG = len(GROUPS)
 TILE = 256
-UNIT = 4
+EARLY, UNIT = 2, 4
 
 ORDER = (
-    ("as", 0, 0), ("as", 1, 0), ("as", 2, 0), ("as", 3, 0), ("as", 4, 0), ("a2a",), ("as", 0, 1), ("as", 1, 1),
-    ("as", 4, 1), ("af", 0, 1), ("as", 2, 1), ("af", 1, 1), ("as", 3, 1), ("af", 4, 1), ("ht", 0), ("as", 1, 2),
-    ("wg", 0, 0), ("wg", 0, 1), ("wg", 0, 2), ("as", 0, 2), ("af", 3, 1), ("wg", 0, 3), ("wg", 0, 4), ("af", 2, 1),
-    ("as", 4, 2), ("af", 0, 2), ("af", 1, 2), ("as", 3, 2), ("hp", 1), ("hp", 3), ("ht", 1), ("as", 2, 2),
-    ("ae", 0, 2), ("wg", 1, 0), ("wg", 1, 1), ("wg", 1, 2), ("wg", 1, 3), ("wg", 1, 4), ("ae", 1, 2), ("ht", 3),
-    ("wg", 3, 0), ("wg", 3, 1), ("wg", 3, 2), ("wg", 3, 3), ("wg", 3, 4), ("af", 2, 2), ("af", 3, 2), ("hp", 2),
-    ("ht", 2), ("wg", 2, 0), ("rs", 0, 2), ("wg", 2, 1), ("rs", 1, 2), ("wg", 2, 2), ("rs", 2, 2), ("wg", 2, 3),
-    ("rs", 3, 2), ("wg", 2, 4), ("af", 4, 2), ("rs", 4, 2), ("ae", 2, 2), ("ae", 3, 2), ("rm", 0, 2), ("rm", 1, 2),
-    ("ae", 4, 2), ("hg", 0), ("hg", 1), ("rm", 2, 2), ("rm", 3, 2), ("rm", 4, 2), ("hg", 2), ("hg", 3), ("rs", 0, 1),
-    ("rs", 1, 1), ("rs", 4, 1), ("rm", 1, 1), ("rs", 2, 1), ("rm", 0, 1), ("rs", 1, 0), ("rs", 3, 1), ("rm", 2, 1),
-    ("rm", 4, 1), ("re", 1, 0), ("rs", 0, 0), ("rm", 3, 1), ("rs", 2, 0), ("re", 0, 0), ("rs", 4, 0), ("rs", 3, 0),
-    ("re", 2, 0), ("re", 4, 0), ("re", 3, 0),
+    ("as", 3, 0), ("as", 4, 0), ("as", 2, 0), ("as", 5, 0), ("as", 0, 0), ("as", 3, 1), ("as", 4, 1), ("as", 1, 0),
+    ("as", 2, 1), ("a2a", 0), ("af", 3, 1), ("as", 5, 1), ("ht", 0), ("af", 4, 1), ("af", 2, 1), ("as", 1, 1),
+    ("wg", 0, 3), ("as", 0, 1), ("wg", 0, 5), ("as", 4, 2), ("wg", 0, 2), ("af", 1, 1), ("wg", 0, 0), ("af", 0, 1),
+    ("as", 2, 2), ("wg", 0, 4), ("af", 4, 2), ("a2a", 1), ("af", 5, 1), ("af", 2, 2), ("wg", 0, 1), ("hp", 1),
+    ("hp", 3), ("as", 1, 2), ("as", 0, 2), ("as", 3, 2), ("ht", 1), ("wg", 1, 4), ("wg", 1, 2), ("wg", 1, 0),
+    ("wg", 1, 5), ("af", 0, 2), ("wg", 1, 1), ("wg", 1, 3), ("ht", 3), ("wg", 3, 0), ("wg", 3, 5), ("hp", 2),
+    ("wg", 3, 2), ("af", 1, 2), ("wg", 3, 4), ("af", 3, 2), ("wg", 3, 3), ("wg", 3, 1), ("ht", 2), ("wg", 2, 5),
+    ("wg", 2, 2), ("wg", 2, 1), ("rs", 1, 2), ("rs", 2, 2), ("ae", 4, 2), ("ae", 2, 2), ("wg", 2, 3), ("as", 5, 2),
+    ("wg", 2, 0), ("wg", 2, 4), ("rs", 4, 2), ("ae", 1, 2), ("ae", 3, 2), ("rs", 0, 2), ("ae", 0, 2), ("ha", 0),
+    ("ha", 1), ("af", 5, 2), ("rs", 3, 2), ("ha", 2), ("ha", 3), ("ha", 4), ("ha", 5), ("ae", 5, 2), ("ha", 6),
+    ("ha", 7), ("rs", 5, 2), ("hb", 0), ("rm", 2, 2), ("hb", 1), ("rm", 1, 2), ("hb", 2), ("hb", 3), ("rm", 0, 2),
+    ("rm", 3, 2), ("rm", 4, 2), ("rm", 5, 2), ("rs", 2, 1), ("rs", 1, 1), ("rs", 3, 1), ("rm", 2, 1), ("rs", 0, 1),
+    ("rm", 1, 1), ("rs", 5, 1), ("rs", 4, 1), ("rm", 0, 1), ("rm", 3, 1), ("rs", 2, 0), ("rm", 5, 1), ("rs", 1, 0),
+    ("rm", 4, 1), ("re", 2, 0), ("rs", 0, 0), ("rs", 5, 0), ("rs", 3, 0), ("re", 1, 0), ("rs", 4, 0), ("re", 5, 0),
+    ("re", 3, 0), ("re", 0, 0), ("re", 4, 0),
 )
 
 
@@ -61,6 +72,7 @@
     tsm = next(it)
     hsend = next(it)
     hrecv = next(it)
+    acc = next(it)
     fin = next(it)
     wgs = next(it)
     ag_s, ag_r, rs_s, rs_r = next(it), next(it), next(it), next(it)
@@ -92,8 +104,22 @@
     peers += [near(axis, 2) for axis in sorted({X} | {order[0] for _, order in GROUPS})] + [other]
     for peer in peers:
         pl.semaphore_signal(barrier, inc=1, device_id=peer, device_id_type=MESH)
+
+    def cols(who):
+        return pl.ds(pl.multiple_of(who * HALF, HALF), HALF)
+
+    def seg(who, n):
+        return pl.ds(pl.multiple_of(who * CAP * BLOCK, CAP * BLOCK), n)
+
+    SEGR = CAP * BLOCK
+    w_local = pltpu.make_async_copy(mw_hbm.at[0, :, cols(c)], wbuf.at[c], loc.at[0])
+    w_local.start()
     bt_local = pltpu.make_async_copy(bt_hbm, bt_ref, loc.at[4])
     bt_local.start()
+    h_local = pltpu.make_async_copy(sh_hbm.at[seg(x, SEGR)], hid.at[c, x], loc.at[1])
+    h_local.start()
+    og_local = pltpu.make_async_copy(og_hbm.at[:, :, cols(c)], og.at[c], loc.at[2])
+    og_local.start()
     pl.semaphore_wait(barrier, len(peers))
 
     sent = []
@@ -109,24 +135,14 @@
         sent.append(copy)
         return copy
 
-    def cols(who):
-        return pl.ds(pl.multiple_of(who * HALF, HALF), HALF)
-
-    def seg(who, n):
-        return pl.ds(pl.multiple_of(who * CAP * BLOCK, CAP * BLOCK), n)
-
-    SEGR = CAP * BLOCK
-    w_local = pltpu.make_async_copy(mw_hbm.at[0, :, cols(c)], wbuf.at[c], loc.at[0])
-    w_local.start()
     w_peer = push(mw_hbm.at[0, :, cols(oc)], wbuf.at[c], ms.at[0], mr.at[0], other)
-    h_local = pltpu.make_async_copy(sh_hbm.at[seg(x, SEGR)], hid.at[c, x], loc.at[1])
-    h_local.start()
     bt_local.wait()
-    tgt[c] = jnp.broadcast_to(bt_ref[...], (BLOCKS, 128))
+    tgt[c] = jnp.zeros((BLOCKS, 128), jnp.int32)
+    tgt[c, :, 0:BLOCKS] = jnp.broadcast_to(bt_ref[...], (BLOCKS, BLOCKS))
     push(tgt.at[c], tgt.at[c], ms.at[1], mr.at[1], other)
 
-    def a2a():
-        for i, delta in enumerate((1, -1, 2)):
+    def a2a(far):
+        for i, delta in ((2, 2),) if far else ((0, 1), (1, -1)):
             push(sh_hbm.at[seg(wrap(x + delta), SEGR)], hid.at[c, x], hs.at[i], hr.at[i], near(X, delta))
 
     def hid_push(k):
@@ -193,9 +209,6 @@
     for g, (width, _) in enumerate(GROUPS):
         rows = wbuf[:, :, OFFSETS[g] : OFFSETS[g] + width].reshape(ROWS, width)
         w[g][x, z, y] = rows.astype(BF16)
-
-    og_local = pltpu.make_async_copy(og_hbm.at[:, :, cols(c)], og.at[c], loc.at[2])
-    og_local.start()
     push(og_hbm.at[:, :, cols(oc)], og.at[c], ms.at[2], mr.at[2], other)
     push(sh_hbm.at[seg(x, SEGR)], hid.at[c, x], hcs.at[0], hcr.at[0], other)
 
@@ -218,7 +231,7 @@
             index = [jnp.int32(0)] * CAP
             valid = [jnp.int32(0)] * CAP
             for b in range(BLOCKS):
-                hit = (tsm[core, b, 0] == t).astype(jnp.int32)
+                hit = (tsm[core, 0, b] == t).astype(jnp.int32)
                 for r in range(CAP):
                     here = hit * (count == r).astype(jnp.int32)
                     index[r] = index[r] + b * here
@@ -326,33 +339,43 @@
         add_in(g, p, m, 0, ((0, 2), (1, 1)))
         add_in(g, p, m, 1, ((0, 1), (1, 2)))
 
-    def half_product(k, b):
-        t = tsm[k, b, 0]
+    def half_product(k, b, groups):
+        t = tsm[k, 0, b]
         acc = jnp.zeros((BLOCK, FF), F32)
-        for g, (width, _) in enumerate(GROUPS):
+        for g in groups:
+            width = GROUPS[g][0]
             lhs = og[k, b, :, OFFSETS[g] : OFFSETS[g] + width]
             rhs = w[g][t].reshape(FF, width)
             acc = acc + lax.dot_general(lhs, rhs, (((1,), (1,)), ((), ())), preferred_element_type=F32)
         return acc
 
-    def for_peer(b, carry):
-        hsend[b] = half_product(oc, b).astype(BF16)
-        remote(hsend.at[b], hrecv.at[b], hps.at[b], hpr.at[b], other).start()
-        return carry
-
-    def for_me(b, carry):
-        acc = half_product(c, b)
-        remote(hsend.at[b], hrecv.at[b], hps.at[b], hpr.at[b], other).wait_recv()
-        hrecv[b] = ((acc + hrecv[b].astype(F32)) * (D**-0.5)).astype(BF16)
-        pltpu.make_async_copy(hrecv.at[b], hg_hbm.at[b], hos.at[b]).start()
-        return carry
-
-    def hidden_grad(u):
+    def hidden_early(u):
+        start = u * EARLY
+        who, start = (oc, start) if start < BLOCKS else (c, start - BLOCKS)
+
+        def one(b, carry):
+            acc[who, b] = half_product(who, b, range(NG - LATE))
+            return carry
+
+        lax.fori_loop(start, start + EARLY, one, 0)
+
+    def hidden_late(u):
         start = u * UNIT
-        if start < BLOCKS:
-            lax.fori_loop(start, start + UNIT, for_peer, 0)
-        else:
-            lax.fori_loop(start - BLOCKS, start - BLOCKS + UNIT, for_me, 0)
+        who, start = (oc, start) if start < BLOCKS else (c, start - BLOCKS)
+
+        def one(b, carry):
+            total = acc[who, b] + half_product(who, b, range(NG - LATE, NG))
+            hop = remote(hsend.at[b], hrecv.at[b], hps.at[b], hpr.at[b], other)
+            if u * UNIT < BLOCKS:
+                hsend[b] = total.astype(BF16)
+                hop.start()
+            else:
+                hop.wait_recv()
+                hrecv[b] = ((total + hrecv[b].astype(F32)) * (D**-0.5)).astype(BF16)
+                pltpu.make_async_copy(hrecv.at[b], hg_hbm.at[b], hos.at[b]).start()
+            return carry
+
+        lax.fori_loop(start, start + UNIT, one, 0)
 
     steps = {
         "as": ag_start,
@@ -365,7 +388,8 @@
         "rs": rs_start,
         "rm": rs_middle,
         "re": rs_finish,
-        "hg": hidden_grad,
+        "ha": hidden_early,
+        "hb": hidden_late,
     }
     for name, *where in ORDER:
         steps[name](*where)
@@ -389,7 +413,7 @@
 
 
 def exchange(out_grad, block_target, saved_hidden, master_weight):
-    scratch = [pltpu.VMEM((BLOCKS, 1), jnp.int32), pltpu.VMEM((2, BLOCKS, BLOCK, HALF), BF16)]
+    scratch = [pltpu.VMEM((1, BLOCKS), jnp.int32), pltpu.VMEM((2, BLOCKS, BLOCK, HALF), BF16)]
     for _ in range(2):
         scratch += [pltpu.VMEM((RING, RING, RING, ROWS, width), BF16) for width, _ in GROUPS]
     for width, _ in GROUPS:
@@ -404,6 +428,7 @@
         pltpu.SMEM((2, BLOCKS, 128), jnp.int32),
         pltpu.VMEM((BLOCKS, BLOCK, FF), BF16),
         pltpu.VMEM((BLOCKS, BLOCK, FF), BF16),
+        pltpu.VMEM((2, BLOCKS, BLOCK, FF), F32),
         pltpu.VMEM((ROWS, HALF), F32),
         pltpu.VMEM((ROWS // 2, D), F32),
         dma((NG, 3, 2, 3)),
@@ -435,7 +460,7 @@
             collective_id=0, has_side_effects=True, vmem_limit_bytes=63 * 1024 * 1024
         ),
         cost_estimate=pl.CostEstimate(flops=20 * 10**9, bytes_accessed=16 * 2**20, transcendentals=0),
-    )(out_grad.reshape(BLOCKS, BLOCK, D), block_target, saved_hidden, master_weight)
+    )(out_grad.reshape(BLOCKS, BLOCK, D), block_target.reshape(1, BLOCKS), saved_hidden, master_weight)
 
 
 def body(out_grad, block_target, saved_hidden, master_weight, first_moment, second_moment):

time: 140 us -> 135 us (0.964)
  Pallas kernels: 135 us -> 130 us
    pallas_call x1, Pallas kernels: 135 us -> 130 us  [exchange(): pl.pallas_call(kernel, out_shape=(jax.ShapeDtypeStruct((BLOCKS, BLOCK, FF...]
where the time goes in v3:
time: 135 us
  Pallas kernels  130 us (96%)
  other arithmetic  2.39 us (2%)
    pallas_call x1, Pallas kernels, exchange(): pl.pallas_call(kernel, out_shape=(jax.ShapeDtypeStruct((BLOCKS, BLOCK, FF...  130 us

profile of v3, /device:TPU:1, one launch (start us, length us, event | category | flops | bytes accessed | tf_op | source)
XLA Modules:
  0.0 134.6 jit_solution(12712038005145371183)
XLA Ops:
  0.6 0.0 copy-start.1
  0.6 0.0 copy-start.2
  0.7 130.4 %shard_map.93 = (bf16[8,128,768]{2,1,0:T(8,128)(2,1)}, f32[24,4096]{1,0:T(8,128)}) custom-call(bf16[8,128,4096]{2,1,0:T(8,128)(2,1)} %bitcast.10, s32[1,8]{1,0:T(1,128)} %bitcast.11, bf16[2048,768]{1,0:T(8,128)(2,1)} %sh_hbm.1, f32[1,24,4096]{2,1,0:T(8,128)} %mw_hbm.1), custom_call_target="tpu_custom_call" | custom-call | flops 20000000000 | bytes 16777216 | tf_op jit(solution)/shard_map/pallas_call | solution.py:450
  131.0 0.0 copy-start
  131.1 0.0 copy-done.1
  131.1 0.0 copy-done.2
  131.1 2.4 %divide_subtract_fusion = (f32[1,24,4096]{2,1,0:T(8,128)}, f32[1,24,4096]{2,1,0:T(8,128)}, f32[1,24,4096]{2,1,0:T(8,128)}) fusion(f32[1,24,4096]{2,1,0:T(8,128)S(1)} %copy-done.1, f32[24,4096]{1,0:T(8,128)} %get-tuple-element.7, f32[1,24,4096]{2,1,0:T(8,128)S(1)} %copy-done.2, f32[1,24,4096]{2,1,0:T(8,128)} %param.11), kind=kLoop, calls=%fused_computation.2 | loop fusion | flops 1277952 | bytes 2752512 | tf_op jit(solution)/shard_map/sub | solution.py:474
  133.5 0.0 copy-done
  133.5 1.1 copy.11
Async XLA Ops:
  0.6 130.4 %copy-start.1 = (f32[1,24,4096]{2,1,0:T(8,128)S(1)}, f32[1,24,4096]{2,1,0:T(8,128)}, u32[]{:S(2)}) copy-start(f32[1,24,4096]{2,1,0:T(8,128)} %mw_hbm.1) | copy-start | bytes 1179652
  0.6 130.4 %copy-start.2 = (f32[1,24,4096]{2,1,0:T(8,128)S(1)}, f32[1,24,4096]{2,1,0:T(8,128)}, u32[]{:S(2)}) copy-start(f32[1,24,4096]{2,1,0:T(8,128)} %param.10) | copy-start | bytes 1179652
  131.0 2.4 %copy-start = (bf16[8,128,768]{2,1,0:T(8,128)(2,1)S(1)}, bf16[8,128,768]{2,1,0:T(8,128)(2,1)}, u32[]{:S(2)}) copy-start(bf16[8,128,768]{2,1,0:T(8,128)(2,1)} %get-tuple-element.6) | copy-start | bytes 4718596

commit v4 on v3

--- a/solution.py
+++ b/solution.py
@@ -40,21 +40,21 @@
 EARLY, UNIT = 2, 4
 
 ORDER = (
-    ("as", 3, 0), ("as", 4, 0), ("as", 2, 0), ("as", 5, 0), ("as", 0, 0), ("as", 3, 1), ("as", 4, 1), ("as", 1, 0),
-    ("as", 2, 1), ("a2a", 0), ("af", 3, 1), ("as", 5, 1), ("ht", 0), ("af", 4, 1), ("af", 2, 1), ("as", 1, 1),
-    ("wg", 0, 3), ("as", 0, 1), ("wg", 0, 5), ("as", 4, 2), ("wg", 0, 2), ("af", 1, 1), ("wg", 0, 0), ("af", 0, 1),
-    ("as", 2, 2), ("wg", 0, 4), ("af", 4, 2), ("a2a", 1), ("af", 5, 1), ("af", 2, 2), ("wg", 0, 1), ("hp", 1),
-    ("hp", 3), ("as", 1, 2), ("as", 0, 2), ("as", 3, 2), ("ht", 1), ("wg", 1, 4), ("wg", 1, 2), ("wg", 1, 0),
-    ("wg", 1, 5), ("af", 0, 2), ("wg", 1, 1), ("wg", 1, 3), ("ht", 3), ("wg", 3, 0), ("wg", 3, 5), ("hp", 2),
-    ("wg", 3, 2), ("af", 1, 2), ("wg", 3, 4), ("af", 3, 2), ("wg", 3, 3), ("wg", 3, 1), ("ht", 2), ("wg", 2, 5),
-    ("wg", 2, 2), ("wg", 2, 1), ("rs", 1, 2), ("rs", 2, 2), ("ae", 4, 2), ("ae", 2, 2), ("wg", 2, 3), ("as", 5, 2),
-    ("wg", 2, 0), ("wg", 2, 4), ("rs", 4, 2), ("ae", 1, 2), ("ae", 3, 2), ("rs", 0, 2), ("ae", 0, 2), ("ha", 0),
-    ("ha", 1), ("af", 5, 2), ("rs", 3, 2), ("ha", 2), ("ha", 3), ("ha", 4), ("ha", 5), ("ae", 5, 2), ("ha", 6),
-    ("ha", 7), ("rs", 5, 2), ("hb", 0), ("rm", 2, 2), ("hb", 1), ("rm", 1, 2), ("hb", 2), ("hb", 3), ("rm", 0, 2),
-    ("rm", 3, 2), ("rm", 4, 2), ("rm", 5, 2), ("rs", 2, 1), ("rs", 1, 1), ("rs", 3, 1), ("rm", 2, 1), ("rs", 0, 1),
-    ("rm", 1, 1), ("rs", 5, 1), ("rs", 4, 1), ("rm", 0, 1), ("rm", 3, 1), ("rs", 2, 0), ("rm", 5, 1), ("rs", 1, 0),
-    ("rm", 4, 1), ("re", 2, 0), ("rs", 0, 0), ("rs", 5, 0), ("rs", 3, 0), ("re", 1, 0), ("rs", 4, 0), ("re", 5, 0),
-    ("re", 3, 0), ("re", 0, 0), ("re", 4, 0),
+    ("as", 4, 0), ("as", 3, 0), ("as", 0, 0), ("as", 5, 0), ("as", 2, 0), ("as", 1, 0), ("as", 4, 1), ("as", 3, 1),
+    ("a2a", 0), ("as", 5, 1), ("as", 0, 1), ("af", 4, 1), ("ht", 0), ("as", 1, 1), ("a2a", 1), ("af", 3, 1),
+    ("af", 0, 1), ("wg", 0, 3), ("af", 5, 1), ("as", 2, 1), ("wg", 0, 4), ("af", 1, 1), ("as", 4, 2), ("as", 0, 2),
+    ("af", 2, 1), ("wg", 0, 0), ("wg", 0, 2), ("wg", 0, 1), ("as", 1, 2), ("hp", 1), ("as", 2, 2), ("wg", 0, 5),
+    ("as", 3, 2), ("af", 0, 2), ("ht", 1), ("hp", 3), ("wg", 1, 2), ("wg", 1, 3), ("wg", 1, 1), ("wg", 1, 4),
+    ("wg", 1, 5), ("wg", 1, 0), ("af", 2, 2), ("af", 1, 2), ("ht", 3), ("wg", 3, 3), ("wg", 3, 1), ("wg", 3, 2),
+    ("af", 4, 2), ("hp", 2), ("wg", 3, 5), ("wg", 3, 0), ("wg", 3, 4), ("af", 3, 2), ("ht", 2), ("wg", 2, 4),
+    ("wg", 2, 1), ("wg", 2, 0), ("wg", 2, 5), ("rs", 0, 2), ("rs", 1, 2), ("wg", 2, 2), ("rs", 4, 2), ("as", 5, 2),
+    ("wg", 2, 3), ("ae", 2, 2), ("ae", 4, 2), ("ae", 3, 2), ("ae", 0, 2), ("ae", 1, 2), ("rs", 3, 2), ("ha", 0),
+    ("ha", 1), ("ha", 2), ("ha", 3), ("af", 5, 2), ("rm", 0, 2), ("ha", 4), ("rs", 2, 2), ("ha", 5), ("rs", 5, 2),
+    ("ha", 6), ("ha", 7), ("rm", 1, 2), ("ae", 5, 2), ("hb", 0), ("hb", 1), ("hb", 2), ("hb", 3), ("rm", 5, 2),
+    ("rs", 0, 1), ("rm", 3, 2), ("rm", 2, 2), ("rm", 4, 2), ("rs", 1, 1), ("rm", 0, 1), ("rs", 5, 1), ("rs", 2, 1),
+    ("rm", 1, 1), ("rs", 3, 1), ("rs", 4, 1), ("rs", 0, 0), ("rm", 2, 1), ("rm", 5, 1), ("rs", 1, 0), ("rm", 3, 1),
+    ("rm", 4, 1), ("rs", 5, 0), ("rs", 2, 0), ("rs", 3, 0), ("rs", 4, 0), ("re", 0, 0), ("re", 5, 0), ("re", 2, 0),
+    ("re", 1, 0), ("re", 3, 0), ("re", 4, 0),
 )
 
 
@@ -80,6 +80,7 @@
     ms, mr = next(it), next(it)
     loc = next(it)
     hps, hpr, hos = next(it), next(it), next(it)
+    fs, fr = next(it), next(it)
 
     x = lax.axis_index("ep")
     e = lax.axis_index("edp")
@@ -258,6 +259,16 @@
 
         lax.fori_loop(0, width // TILE, tile, 0)
 
+    def rows_of(who):
+        return pl.ds(pl.multiple_of(who * (ROWS // 2), 8), ROWS // 2)
+
+    def span_of(half, g):
+        return pl.ds(pl.multiple_of(half * HALF, HALF) + OFFSETS[g], GROUPS[g][0])
+
+    def fin_hop(g, half, rows):
+        src = fin.at[rows_of(rows), OFFSETS[g] : OFFSETS[g] + GROUPS[g][0]]
+        return (src, wgs.at[:, span_of(half, g)], fs.at[g], fr.at[g], other)
+
     def rs_copy(g, p, d, k, q, h):
         return remote(
             block(part[g], g, p, q, h),
@@ -332,6 +343,8 @@
                 rs_direct(g, k, m).wait_recv()
                 total = total + land[g][0][k].astype(F32)
             fin[:, OFFSETS[g] : OFFSETS[g] + GROUPS[g][0]] = total
+            push(*fin_hop(g, c, oc))
+            wgs[:, span_of(c, g)] = fin[rows_of(c), OFFSETS[g] : OFFSETS[g] + GROUPS[g][0]]
             return
         for k in (1, 2):
             for d in range(2):
@@ -394,12 +407,8 @@
     for name, *where in ORDER:
         steps[name](*where)
 
-    def rows_of(who):
-        return pl.ds(pl.multiple_of(who * (ROWS // 2), 8), ROWS // 2)
-
-    push(fin.at[rows_of(oc)], wgs.at[:, cols(c)], ms.at[3], mr.at[3], other)
-    wgs[:, cols(c)] = fin[rows_of(c), :]
-    remote(fin.at[rows_of(c)], wgs.at[:, cols(oc)], ms.at[3], mr.at[3], other).wait_recv()
+    for g in range(NG):
+        remote(*fin_hop(g, oc, c)).wait_recv()
     wg_ref[...] = wgs[...]
 
     def drain(b, carry):
@@ -445,6 +454,8 @@
         dma((BLOCKS,)),
         dma((BLOCKS,)),
         dma((BLOCKS,)),
+        dma((NG,)),
+        dma((NG,)),
     ]
     anywhere = pl.BlockSpec(memory_space=pl.ANY)
     return pl.pallas_call(

time: 135 us -> 133 us (0.985)
    pallas_call x1, Pallas kernels: 130 us -> 129 us  [exchange(): pl.pallas_call(kernel, out_shape=(jax.ShapeDtypeStruct((BLOCKS, BLOCK, FF...]
where the time goes in v4:
time: 133 us
  Pallas kernels  129 us (97%)
  other arithmetic  2.39 us (2%)
    pallas_call x1, Pallas kernels, exchange(): pl.pallas_call(kernel, out_shape=(jax.ShapeDtypeStruct((BLOCKS, BLOCK, FF...  129 us

profile of v4, /device:TPU:1, one launch (start us, length us, event | category | flops | bytes accessed | tf_op | source)
XLA Modules:
  0.0 132.7 jit_solution(14645337775872464697)
XLA Ops:
  0.6 0.0 copy-start.1
  0.6 0.0 copy-start.2
  0.7 128.5 %shard_map.93 = (bf16[8,128,768]{2,1,0:T(8,128)(2,1)}, f32[24,4096]{1,0:T(8,128)}) custom-call(bf16[8,128,4096]{2,1,0:T(8,128)(2,1)} %bitcast.10, s32[1,8]{1,0:T(1,128)} %bitcast.11, bf16[2048,768]{1,0:T(8,128)(2,1)} %sh_hbm.1, f32[1,24,4096]{2,1,0:T(8,128)} %mw_hbm.1), custom_call_target="tpu_custom_call" | custom-call | flops 20000000000 | bytes 16777216 | tf_op jit(solution)/shard_map/pallas_call | solution.py:461
  129.2 0.0 copy-start
  129.2 0.0 copy-done.1
  129.2 0.0 copy-done.2
  129.2 2.4 %divide_subtract_fusion = (f32[1,24,4096]{2,1,0:T(8,128)}, f32[1,24,4096]{2,1,0:T(8,128)}, f32[1,24,4096]{2,1,0:T(8,128)}) fusion(f32[1,24,4096]{2,1,0:T(8,128)S(1)} %copy-done.1, f32[24,4096]{1,0:T(8,128)} %get-tuple-element.7, f32[1,24,4096]{2,1,0:T(8,128)S(1)} %copy-done.2, f32[1,24,4096]{2,1,0:T(8,128)} %param.11), kind=kLoop, calls=%fused_computation.2 | loop fusion | flops 1277952 | bytes 2752512 | tf_op jit(solution)/shard_map/sub | solution.py:485
  131.6 0.0 copy-done
  131.6 1.1 copy.11
Async XLA Ops:
  0.6 128.6 %copy-start.1 = (f32[1,24,4096]{2,1,0:T(8,128)S(1)}, f32[1,24,4096]{2,1,0:T(8,128)}, u32[]{:S(2)}) copy-start(f32[1,24,4096]{2,1,0:T(8,128)} %mw_hbm.1) | copy-start | bytes 1179652
  0.6 128.6 %copy-start.2 = (f32[1,24,4096]{2,1,0:T(8,128)S(1)}, f32[1,24,4096]{2,1,0:T(8,128)}, u32[]{:S(2)}) copy-start(f32[1,24,4096]{2,1,0:T(8,128)} %param.10) | copy-start | bytes 1179652
  129.2 2.4 %copy-start = (bf16[8,128,768]{2,1,0:T(8,128)(2,1)S(1)}, bf16[8,128,768]{2,1,0:T(8,128)(2,1)}, u32[]{:S(2)}) copy-start(bf16[8,128,768]{2,1,0:T(8,128)(2,1)} %get-tuple-element.6) | copy-start | bytes 4718596

commit v5 on v4

--- a/solution.py
+++ b/solution.py
@@ -41,9 +41,9 @@
 
 ORDER = (
     ("as", 4, 0), ("as", 3, 0), ("as", 0, 0), ("as", 5, 0), ("as", 2, 0), ("as", 1, 0), ("as", 4, 1), ("as", 3, 1),
-    ("a2a", 0), ("as", 5, 1), ("as", 0, 1), ("af", 4, 1), ("ht", 0), ("as", 1, 1), ("a2a", 1), ("af", 3, 1),
-    ("af", 0, 1), ("wg", 0, 3), ("af", 5, 1), ("as", 2, 1), ("wg", 0, 4), ("af", 1, 1), ("as", 4, 2), ("as", 0, 2),
-    ("af", 2, 1), ("wg", 0, 0), ("wg", 0, 2), ("wg", 0, 1), ("as", 1, 2), ("hp", 1), ("as", 2, 2), ("wg", 0, 5),
+    ("a2a", 0), ("as", 5, 1), ("as", 0, 1), ("af", 4, 1), ("as", 1, 1), ("a2a", 1), ("af", 3, 1), ("af", 0, 1),
+    ("af", 5, 1), ("as", 2, 1), ("af", 1, 1), ("as", 4, 2), ("as", 0, 2), ("af", 2, 1), ("as", 1, 2), ("ht", 0),
+    ("wg", 0, 3), ("wg", 0, 4), ("wg", 0, 0), ("wg", 0, 2), ("wg", 0, 1), ("hp", 1), ("as", 2, 2), ("wg", 0, 5),
     ("as", 3, 2), ("af", 0, 2), ("ht", 1), ("hp", 3), ("wg", 1, 2), ("wg", 1, 3), ("wg", 1, 1), ("wg", 1, 4),
     ("wg", 1, 5), ("wg", 1, 0), ("af", 2, 2), ("af", 1, 2), ("ht", 3), ("wg", 3, 3), ("wg", 3, 1), ("wg", 3, 2),
     ("af", 4, 2), ("hp", 2), ("wg", 3, 5), ("wg", 3, 0), ("wg", 3, 4), ("af", 3, 2), ("ht", 2), ("wg", 2, 4),
@@ -58,7 +58,7 @@
 )
 
 
-def kernel(og_hbm, bt_hbm, sh_hbm, mw_hbm, hg_hbm, wg_ref, *scratch):
+def kernel(og_hbm, bt_hbm, sh_hbm, mw_hbm, hg_hbm, wg_hbm, *scratch):
     it = iter(scratch)
     bt_ref = next(it)
     og = next(it)
@@ -80,7 +80,7 @@
     ms, mr = next(it), next(it)
     loc = next(it)
     hps, hpr, hos = next(it), next(it), next(it)
-    fs, fr = next(it), next(it)
+    fs, fr, ws = next(it), next(it), next(it)
 
     x = lax.axis_index("ep")
     e = lax.axis_index("edp")
@@ -103,7 +103,7 @@
     barrier = pltpu.get_barrier_semaphore()
     peers = [near(axis, delta) for axis in (X, Z, Y) for delta in (1, -1)]
     peers += [near(axis, 2) for axis in sorted({X} | {order[0] for _, order in GROUPS})] + [other]
-    for peer in peers:
+    for peer in peers[::-1]:
         pl.semaphore_signal(barrier, inc=1, device_id=peer, device_id_type=MESH)
 
     def cols(who):
@@ -269,6 +269,9 @@
         src = fin.at[rows_of(rows), OFFSETS[g] : OFFSETS[g] + GROUPS[g][0]]
         return (src, wgs.at[:, span_of(half, g)], fs.at[g], fr.at[g], other)
 
+    def store(g, i, half):
+        return pltpu.make_async_copy(wgs.at[:, span_of(half, g)], wg_hbm.at[:, span_of(half, g)], ws.at[i, g])
+
     def rs_copy(g, p, d, k, q, h):
         return remote(
             block(part[g], g, p, q, h),
@@ -345,6 +348,7 @@
             fin[:, OFFSETS[g] : OFFSETS[g] + GROUPS[g][0]] = total
             push(*fin_hop(g, c, oc))
             wgs[:, span_of(c, g)] = fin[rows_of(c), OFFSETS[g] : OFFSETS[g] + GROUPS[g][0]]
+            store(g, 0, c).start()
             return
         for k in (1, 2):
             for d in range(2):
@@ -407,9 +411,13 @@
     for name, *where in ORDER:
         steps[name](*where)
 
-    for g in range(NG):
+    ended = [where[0] for name, *where in ORDER if name == "re"]
+    for g in ended:
         remote(*fin_hop(g, oc, c)).wait_recv()
-    wg_ref[...] = wgs[...]
+        store(g, 1, oc).start()
+    for g in ended:
+        store(g, 0, c).wait()
+        store(g, 1, oc).wait()
 
     def drain(b, carry):
         remote(hsend.at[b], hrecv.at[b], hps.at[b], hpr.at[b], other).wait_send()
@@ -456,6 +464,7 @@
         dma((BLOCKS,)),
         dma((NG,)),
         dma((NG,)),
+        dma((2, NG)),
     ]
     anywhere = pl.BlockSpec(memory_space=pl.ANY)
     return pl.pallas_call(
@@ -465,7 +474,7 @@
             jax.ShapeDtypeStruct((ROWS // 2, D), F32),
         ),
         in_specs=[anywhere] * 4,
-        out_specs=(anywhere, pl.BlockSpec(memory_space=pltpu.VMEM)),
+        out_specs=(anywhere, anywhere),
         scratch_shapes=scratch,
         compiler_params=pltpu.CompilerParams(
             collective_id=0, has_side_effects=True, vmem_limit_bytes=63 * 1024 * 1024

time: 133 us -> 133 us (level)
  no operation moved by 1% of the time
where the time goes in v5:
time: 133 us
  Pallas kernels  128 us (96%)
  other arithmetic  2.39 us (2%)
    pallas_call x1, Pallas kernels, exchange(): pl.pallas_call(kernel, out_shape=(jax.ShapeDtypeStruct((BLOCKS, BLOCK, FF...  128 us

profile of v5, /device:TPU:1, one launch (start us, length us, event | category | flops | bytes accessed | tf_op | source)
XLA Modules:
  0.0 132.6 jit_solution(10636047207734266755)
XLA Ops:
  0.6 0.0 copy-start.1
  0.6 0.0 copy-start.2
  0.7 128.4 %shard_map.93 = (bf16[8,128,768]{2,1,0:T(8,128)(2,1)}, f32[24,4096]{1,0:T(8,128)}) custom-call(bf16[8,128,4096]{2,1,0:T(8,128)(2,1)} %bitcast.10, s32[1,8]{1,0:T(1,128)} %bitcast.11, bf16[2048,768]{1,0:T(8,128)(2,1)} %sh_hbm.1, f32[1,24,4096]{2,1,0:T(8,128)} %mw_hbm.1), custom_call_target="tpu_custom_call" | custom-call | flops 20000000000 | bytes 16777216 | tf_op jit(solution)/shard_map/pallas_call | solution.py:470
  129.1 0.0 copy-start
  129.1 0.0 copy-done.1
  129.1 0.0 copy-done.2
  129.1 2.4 %divide_subtract_fusion = (f32[1,24,4096]{2,1,0:T(8,128)}, f32[1,24,4096]{2,1,0:T(8,128)}, f32[1,24,4096]{2,1,0:T(8,128)}) fusion(f32[1,24,4096]{2,1,0:T(8,128)S(1)} %copy-done.1, f32[24,4096]{1,0:T(8,128)} %get-tuple-element.7, f32[1,24,4096]{2,1,0:T(8,128)S(1)} %copy-done.2, f32[1,24,4096]{2,1,0:T(8,128)} %param.11), kind=kLoop, calls=%fused_computation.2 | loop fusion | flops 1277952 | bytes 2752512 | tf_op jit(solution)/shard_map/sub | solution.py:494
  131.5 0.0 copy-done
  131.5 1.1 copy.11
Async XLA Ops:
  0.6 128.5 %copy-start.1 = (f32[1,24,4096]{2,1,0:T(8,128)S(1)}, f32[1,24,4096]{2,1,0:T(8,128)}, u32[]{:S(2)}) copy-start(f32[1,24,4096]{2,1,0:T(8,128)} %mw_hbm.1) | copy-start | bytes 1179652
  0.6 128.5 %copy-start.2 = (f32[1,24,4096]{2,1,0:T(8,128)S(1)}, f32[1,24,4096]{2,1,0:T(8,128)}, u32[]{:S(2)}) copy-start(f32[1,24,4096]{2,1,0:T(8,128)} %param.10) | copy-start | bytes 1179652
  129.1 2.4 %copy-start = (bf16[8,128,768]{2,1,0:T(8,128)(2,1)S(1)}, bf16[8,128,768]{2,1,0:T(8,128)(2,1)}, u32[]{:S(2)}) copy-start(bf16[8,128,768]{2,1,0:T(8,128)(2,1)} %get-tuple-element.6) | copy-start | bytes 4718596
